TPU v7x, 32 devices: a whole 2x2x4 slice. The times are simulated.
32 devices in a mesh: axial: 4 (over z), radial: 4 (over y, x), azim: 2 (over core).
Axes of the slice: x: 2, y: 2, z: 4, core: 2. Of those that a mesh axis runs over, the one named last changes fastest.
Arguments:
- source: float32 [3, 64, 64, 256], P(None, 'axial', 'radial', 'azim'), may hold values from -6 to 6
- region: int32 [64, 64, 256], P('axial', 'radial', 'azim'), may hold values from 0 to 401
- fixed_flags: int32 [64, 64, 256], P('axial', 'radial', 'azim'), may hold values 0 or 1
- reluctivity_table: float32 [402], replicated, may hold values from 0.5 to 4
- conductivity_table: float32 [402], replicated, may hold values from 0.5 to 4
Outputs:
- solution: float32 [3, 64, 64, 256], P(None, 'axial', 'radial', 'azim')
- residual: float32 [3, 64, 64, 256], P(None, 'axial', 'radial', 'azim')
All inputs are finite; a program needn't handle non-finite values. No bound on the sum of `fixed_flags` on one device may be relied on, other than what follows from the above.
Results may differ from a plain program's by a relative error of at most 0.0003.
Values sent between devices are 32-bit elements; how exact they have to be, the bound alone decides.
A program may use at most 64 MiB of HBM per device.

v0:
```python
import jax
import jax.numpy as jnp
from jax import lax
from jax.sharding import PartitionSpec as P

BA = 8
CYCLES = 2
NS = 2
ES = 2


relax_edge = 0.4
relax_node = 0.6
ground_share = 0.01


def from_behind(x, axis, by):
    devices = lax.axis_size(axis)
    pairs = [(i, i + by) for i in range(devices) if 0 <= i + by < devices]
    return lax.ppermute(x, axis, pairs)


def from_behind_2(x, axis, by):
    devices = lax.axis_size(axis)
    return lax.ppermute(x, axis, [(i, (i + by) % devices) for i in range(devices)])


def with_halo(cells, sides, width, closed):
    for axis, dim in sides:
        count = lax.axis_size(axis)
        ends = count if closed else count - 1
        head = lax.slice_in_dim(cells, 0, width, axis=dim)
        tail = lax.slice_in_dim(cells, cells.shape[dim] - width, cells.shape[dim], axis=dim)
        cells = jnp.concatenate(
            [
                lax.ppermute(tail, axis, [(i, (i + 1) % count) for i in range(ends)]),
                cells,
                lax.ppermute(head, axis, [((i + 1) % count, i) for i in range(ends)]),
            ],
            axis=dim,
        )
    return cells


def prefix(value, axis, join, neutral, backward):
    count, mine = (lax.axis_size(axis), lax.axis_index(axis))
    pieces = jax.tree.map(lambda part: lax.all_gather(part, axis), value)
    if backward:
        pieces = jax.tree.map(lambda part: part[::-1], pieces)
        mine = count - 1 - mine
    running = jax.tree.map(
        lambda part, zero: jnp.full_like(part, 0) + jnp.asarray(zero, part.dtype), value, neutral
    )

    def turn(position, running):
        longer = join(running, jax.tree.map(lambda part: part[position], pieces))
        return jax.tree.map(lambda new, old: jnp.where(position < mine, new, old), longer, running)

    return lax.fori_loop(0, count - 1, turn, running)


def unit_step(direction, chosen, elsewhere):
    return tuple((chosen if position == direction else elsewhere for position in range(3)))


def window(values, low_cuts, high_cuts):
    extent = values.shape[-3:]
    return values[
        ...,
        low_cuts[0] : extent[0] - high_cuts[0],
        low_cuts[1] : extent[1] - high_cuts[1],
        low_cuts[2] : extent[2] - high_cuts[2],
    ]


def forward_diff(values, direction):
    return window(values, unit_step(direction, 1, 0), unit_step(direction, 0, 1)) - window(
        values, (0, 0, 0), (1, 1, 1)
    )


def adjoint_diff(values, direction):
    return window(values, unit_step(direction, 0, 1), unit_step(direction, 1, 0)) - window(
        values, (1, 1, 1), (0, 0, 0)
    )


def apply_operator(padded, reluct_pad, conduct_pad, free_pad):
    face_zero = forward_diff(padded[2], 1) - forward_diff(padded[1], 2)
    face_one = forward_diff(padded[0], 2) - forward_diff(padded[2], 0)
    face_two = forward_diff(padded[1], 0) - forward_diff(padded[0], 1)
    weight = window(reluct_pad, (0, 0, 0), (1, 1, 1))
    field_zero = weight * face_zero
    field_one = weight * face_one
    field_two = weight * face_two
    curl_zero = adjoint_diff(field_one, 2) - adjoint_diff(field_two, 1)
    curl_one = adjoint_diff(field_two, 0) - adjoint_diff(field_zero, 2)
    curl_two = adjoint_diff(field_zero, 1) - adjoint_diff(field_one, 0)
    centred = window(padded, (1, 1, 1), (1, 1, 1))
    result = (
        jnp.stack([curl_zero, curl_one, curl_two])
        + window(conduct_pad, (1, 1, 1), (1, 1, 1)) * centred
    )
    return result * window(free_pad, (1, 1, 1), (1, 1, 1))


def edge_region_gradient(padded_nodes):
    return jnp.stack([forward_diff(padded_nodes, direction) for direction in range(3)])


def gradient(padded_nodes):
    return window(edge_region_gradient(padded_nodes), (1, 1, 1), (0, 0, 0))


def grad_adjoint(edges):
    return adjoint_diff(edges[0], 0) + adjoint_diff(edges[1], 1) + adjoint_diff(edges[2], 2)


def lower_shift(values, direction):
    return window(values, unit_step(direction, 0, 1), unit_step(direction, 2, 1))


def inverse_diag(reluct_big, conduct_here, free_here):
    centre = window(reluct_big, (1, 1, 1), (1, 1, 1))
    lower_zero = lower_shift(reluct_big, 0)
    lower_one = lower_shift(reluct_big, 1)
    lower_two = lower_shift(reluct_big, 2)
    diag_zero = 2.0 * centre + lower_one + lower_two + conduct_here
    diag_one = 2.0 * centre + lower_zero + lower_two + conduct_here
    diag_two = 2.0 * centre + lower_zero + lower_one + conduct_here
    diagonal = jnp.stack([diag_zero, diag_one, diag_two])
    return free_here / (diagonal + 1.0 - free_here)


def node_diag(conduct_big):
    centre = window(conduct_big, (1, 1, 1), (1, 1, 1))
    return (
        3.0 * centre
        + lower_shift(conduct_big, 0)
        + lower_shift(conduct_big, 1)
        + lower_shift(conduct_big, 2)
    )


def trim_pad(values, margin):
    cut_size = 3 - margin
    return window(values, (cut_size, cut_size, cut_size), (cut_size, cut_size, cut_size))


def pad_lower(values):
    axial_layer = from_behind(values[:, -1:], "axial", 1)
    radial_layer = from_behind(values[:, :, -1:], "radial", 1)
    around_layer = from_behind_2(values[:, :, :, -1:], "azim", 1)
    padded = jnp.pad(values, ((0, 0), (3, 3), (3, 3), (3, 3)))
    padded = padded.at[:, 2:3, 3:-3, 3:-3].set(axial_layer)
    padded = padded.at[:, 3:-3, 2:3, 3:-3].set(radial_layer)
    padded = padded.at[:, 3:-3, 3:-3, 2:3].set(around_layer)
    return padded


def pad_edges(values):
    wrapped = with_halo(values, (("azim", 3),), 1, True)
    return with_halo(wrapped, (("axial", 1), ("radial", 2)), 1, False)


def pad_nodes(values):
    wrapped = with_halo(values, (("azim", 2),), 1, True)
    return with_halo(wrapped, (("axial", 0), ("radial", 1)), 1, False)


def combine_pivots(first_map, second_map):
    top_left = second_map[0] * first_map[0] + second_map[1] * first_map[2]
    top_right = second_map[0] * first_map[1] + second_map[1] * first_map[3]
    low_left = second_map[2] * first_map[0] + second_map[3] * first_map[2]
    low_right = second_map[2] * first_map[1] + second_map[3] * first_map[3]
    magnitude = jnp.abs(top_left) + jnp.abs(top_right) + jnp.abs(low_left) + jnp.abs(low_right)
    return (
        top_left / magnitude,
        top_right / magnitude,
        low_left / magnitude,
        low_right / magnitude,
    )


def combine_affine(first_map, second_map):
    return (second_map[0] * first_map[0], second_map[0] * first_map[1] + second_map[1])


def on_device(source, region, fixed_flags, reluctivity_table, conductivity_table):
    axial_cells, radial_cells, around_cells = region.shape
    tables = jnp.stack([reluctivity_table, conductivity_table])
    levels = lax.iota(jnp.int32, tables.shape[1])

    def lookup(row_ids):
        onehot = (levels[:, None] == row_ids[None, :]).astype(jnp.float32)
        return jnp.dot(
            tables, onehot, precision=lax.Precision.HIGHEST, preferred_element_type=jnp.float32
        )

    looked = lax.map(lookup, region.reshape(axial_cells, radial_cells * around_cells))
    looked = jnp.transpose(looked, (1, 0, 2)).reshape(2, axial_cells, radial_cells, around_cells)
    free_mask = (1 - fixed_flags).astype(jnp.float32)
    coefficients = jnp.concatenate([looked, free_mask[None]], axis=0)
    padded_coefs = pad_lower(coefficients)
    reluct_pad = padded_coefs[0]
    conduct_pad = padded_coefs[1]
    free_pad = padded_coefs[2]
    inverse_wide = inverse_diag(
        trim_pad(reluct_pad, ES + 1), trim_pad(conduct_pad, ES), trim_pad(free_pad, ES)
    )
    node_inverse = 1.0 / node_diag(trim_pad(conduct_pad, 1))
    reluct_one = trim_pad(reluct_pad, 1)
    conduct_one = trim_pad(conduct_pad, 1)
    free_one = trim_pad(free_pad, 1)
    node_weight = window(conduct_one * free_one, (0, 0, 0), (1, 1, 1))

    def apply_local(values):
        return apply_operator(pad_edges(values), reluct_one, conduct_one, free_one)

    groups = axial_cells // BA
    conduct_here = trim_pad(conduct_pad, 0)
    conduct_blocks = conduct_here.reshape(groups, BA, radial_cells, around_cells)
    couplings = jnp.sum(conduct_blocks[:, BA - 1], axis=(1, 2))
    grounds = ground_share * jnp.sum(conduct_blocks[:, 0], axis=(1, 2))
    below_sum = jnp.sum(conduct_pad[2, 3:-3, 3:-3])
    lower_coupling = jnp.concatenate([below_sum[None], couplings[:-1]])
    diagonal = lower_coupling + couplings + grounds
    identity_one = jnp.ones((1,), jnp.float32)
    identity_zero = jnp.zeros((1,), jnp.float32)
    device_matrix = (identity_one, identity_zero, identity_zero, identity_one)
    for group_index in range(groups):
        lower_here = lower_coupling[group_index : group_index + 1]
        step_matrix = (
            diagonal[group_index : group_index + 1],
            -lower_here * lower_here,
            identity_one,
            identity_zero,
        )
        device_matrix = combine_pivots(device_matrix, step_matrix)
    incoming = prefix(
        device_matrix,
        "axial",
        combine_pivots,
        (identity_one, identity_zero, identity_zero, identity_one),
        False,
    )
    previous = (incoming[0] + incoming[1]) / (incoming[2] + incoming[3])
    pivot_list = []
    for group_index in range(groups):
        lower_here = lower_coupling[group_index : group_index + 1]
        previous = diagonal[group_index : group_index + 1] - lower_here * lower_here / previous
        pivot_list.append(previous)
    pivots = jnp.concatenate(pivot_list)
    forward_slope = lower_coupling / pivots
    backward_slope = couplings / pivots
    solution = jnp.zeros_like(source)
    residual = free_mask * source
    for cycle_index in range(CYCLES):
        node_res = grad_adjoint(window(pad_edges(residual), (0, 0, 0), (1, 1, 1)))
        potential = jnp.zeros_like(node_res)
        for sweep_index in range(NS):
            change = relax_node * node_inverse * node_res
            potential = potential + change
            node_res = node_res - grad_adjoint(
                node_weight * edge_region_gradient(pad_nodes(change))
            )
        totals = jnp.sum(node_res.reshape(groups, BA * radial_cells * around_cells), axis=1)
        forward_offset = totals / pivots
        slope_now = identity_one
        offset_now = identity_zero
        for coarse_group_index in range(groups):
            slope_here = forward_slope[coarse_group_index : coarse_group_index + 1]
            slope_now = slope_here * slope_now
            offset_now = (
                slope_here * offset_now
                + forward_offset[coarse_group_index : coarse_group_index + 1]
            )
        entering_map = prefix(
            (slope_now, offset_now), "axial", combine_affine, (identity_one, identity_zero), False
        )
        entering = entering_map[1]
        forward_values = []
        running = entering
        for coarse_group_index in range(groups):
            running = (
                forward_slope[coarse_group_index : coarse_group_index + 1] * running
                + forward_offset[coarse_group_index : coarse_group_index + 1]
            )
            forward_values.append(running)
        slope_back = identity_one
        offset_back = identity_zero
        for coarse_group_index in reversed(range(groups)):
            slope_here = backward_slope[coarse_group_index : coarse_group_index + 1]
            slope_back = slope_here * slope_back
            offset_back = slope_here * offset_back + forward_values[coarse_group_index]
        above_map = prefix(
            (slope_back, offset_back), "axial", combine_affine, (identity_one, identity_zero), True
        )
        from_above = above_map[1]
        backward_values = [identity_zero] * groups
        running = from_above
        for coarse_group_index in reversed(range(groups)):
            running = (
                forward_values[coarse_group_index]
                + backward_slope[coarse_group_index : coarse_group_index + 1] * running
            )
            backward_values[coarse_group_index] = running
        lifted = jnp.concatenate(backward_values)
        potential = (
            potential.reshape(groups, BA, radial_cells, around_cells) + lifted[:, None, None, None]
        ).reshape(axial_cells, radial_cells, around_cells)
        correction = gradient(pad_nodes(potential)) * free_mask
        solution = solution + correction
        residual = residual - apply_local(correction)
        inverse = window(inverse_wide, (ES, ES, ES), (ES, ES, ES))
        for sweep_index in range(ES):
            change = relax_edge * inverse * residual
            solution = solution + change
            residual = residual - apply_local(change)
    return (solution, residual)


def solution(mesh):
    placed = (
        P(None, "axial", "radial", "azim"),
        P("axial", "radial", "azim"),
        P("axial", "radial", "azim"),
        P(),
        P(),
    )
    return jax.shard_map(
        on_device,
        mesh=mesh,
        in_specs=placed,
        out_specs=(P(None, "axial", "radial", "azim"), P(None, "axial", "radial", "azim")),
        check_vma=False,
    )
```

profile of v0, /device:TPU:0, one launch (start us, length us, event | category | flops | bytes accessed | tf_op | source)
XLA Modules:
  0.0 462.9 jit_solution(15702017213685471557)
XLA Ops:
  2.3 18.9 %while.90 = (s32[]{:T(128)}, f32[16,2,2048]{2,1,0:T(2,128)S(1)}, s32[16,2048]{1,0:T(8,128)S(1)}, f32[2,402]{1,0:T(2,128)S(1)}, s32[]{:T(128)}) while((s32[]{:T(128)}, f32[16,2,2048]{2,1,0:T(2,128)S(1)}, s32[16,2048]{1,0:T(8,128)S(1)}, f32[2,402]{1,0:T(2,128)S(1)}, s32[]{:T(128)}) %tuple.314), condition=%wide.region_1.2_spmd.clone, body=%wide.region_0.1_spmd.clone.sunk | while | flops 20582400 | bytes 45133 | solution.py:200
  21.5 4.8 %collective-permute-start.1 = (f32[3,16,1,128]{3,2,1,0:T(1,128)S(1)}, f32[3,16,1,128]{3,2,1,0:T(1,128)S(1)}, u32[]{:S(2)}, u32[]{:S(2)}) collective-permute-start(f32[3,16,1,128]{3,2,1,0:T(1,128)S(1)} %fusion.143), channel_id=1, source_target_pairs={{0,2},{2,4},{4,6},{1,3},{3,5},{5,7},{8,10},{10,12},{12,14},{9,11},... | collective-permute-start | bytes 73736 | tf_op jit(solution)/shard_map/ppermute | solution.py:20
  26.3 3.5 collective-permute-start
  36.1 3.5 collective-permute-start.5
  42.6 7.3 %scatter.11 = f32[3,22,22,134]{3,2,1,0:T(8,128)S(1)} dynamic-update-slice(f32[3,22,22,134]{3,2,1,0:T(8,128)S(1)} %scatter.10, f32[3,16,1,128]{3,2,1,0:T(1,128)S(1)} %collective-permute-done.1, s32[]{:T(128)} %copy.85, s32[]{:T(128)} %constant.242.clone.1, s32[]{:T(128)} %constant.241.clone.1, s32[]{:T(128)} %constant.242.clone.1) | dynamic-update-slice | bytes 49156 | tf_op jit(solution)/shard_map/scatter | solution.py:156
  49.9 9.8 %scatter.14 = f32[3,22,22,134]{3,2,1,0:T(8,128)S(1)} dynamic-update-slice(f32[3,22,22,134]{3,2,1,0:T(8,128)S(1)} %scatter.11, f32[3,16,16,1]{3,2,1,0:T(8,128)} %collective-permute-done.2, s32[]{:T(128)} %copy.85, s32[]{:T(128)} %constant.242.clone.1, s32[]{:T(128)} %constant.242.clone.1, s32[]{:T(128)} %constant.241.clone.1) | dynamic-update-slice | bytes 6148 | tf_op jit(solution)/shard_map/scatter | solution.py:157
  62.3 3.4 collective-permute-start.7
  72.3 4.5 collective-permute-start.10
  78.2 3.1 divide_dynamic-update-slice_fusion.3
  82.7 4.3 collective-permute-start.12
  87.0 2.7 divide_dynamic-update-slice_fusion.2
  89.7 2.6 divide_dynamic-update-slice_fusion.1
  92.3 2.7 divide_dynamic-update-slice_fusion
  95.0 10.3 %all-reduce.13 = (f32[4]{0:T(128)S(1)}, f32[4]{0:T(128)S(1)}, f32[4]{0:T(128)S(1)}, f32[4]{0:T(128)S(1)}) all-reduce(f32[4]{0:T(128)S(1)} %get-tuple-element.927, f32[4]{0:T(128)S(1)} %divide_dynamic-update-slice_fusion.2, f32[4]{0:T(128)S(1)} %divide_dynamic-update-slice_fusion.1, ...), channel_id=2, replica_groups=mesh['axial'=4,'radial'=4,'azim'=2] {'axial'}, use_global_device_ids=true, to_apply=%add.1 | all-reduce | flops 16 | bytes 128
  106.8 4.5 collective-permute-done.13
  112.8 18.8 %while.85 = (s32[]{:T(128)}, f32[1]{0:T(128)}, f32[1]{0:T(128)}, f32[1]{0:T(128)}, f32[1]{0:T(128)}, /*index=5*/s32[]{:T(128)}, f32[4,1]{0,1:T(1,128)S(1)}, f32[...) while((s32[]{:T(128)}, f32[1]{0:T(128)}, f32[1]{0:T(128)}, f32[1]{0:T(128)}, ...), condition=%wide.region_6.7_spmd, body=%wide.region_5.6_spmd.sunk | while | flops 30 | bytes 478 | solution.py:59
  131.7 2.1 collective-permute-start.16
  136.3 3.1 collective-permute-done.17
  139.6 4.8 %collective-permute-start.18 = (f32[18,1,130]{2,1,0:T(1,128)S(1)}, f32[18,1,130]{2,1,0:T(1,128)S(1)}, u32[]{:S(2)}, u32[]{:S(2)}) collective-permute-start(f32[18,1,130]{2,1,0:T(1,128)S(1)} %get-tuple-element.856), channel_id=1, source_target_pairs={{0,2},{2,4},{4,6},{1,3},{3,5},{5,7},{8,10},{10,12},{12,14},{9,11},... | collective-permute-start | bytes 28088 | tf_op jit(solution)/shard_map/ppermute | solution.py:36
  147.4 4.1 collective-permute-done.19
  156.5 8.3 %all-reduce.12 = (f32[4]{0:T(128)S(1)}, f32[4]{0:T(128)S(1)}) all-reduce(f32[4]{0:T(128)S(1)} %multiply_dynamic-update-slice_fusion.1, f32[4]{0:T(128)S(1)} %add_dynamic-update-slice_fusion.3), channel_id=6, replica_groups=mesh['axial'=4,'radial'=4,'azim'=2] {'axial'}, use_global_device_ids=true, to_apply=%add.5 | all-reduce | flops 8 | bytes 64
  164.8 5.5 %while.86 = (s32[]{:T(128)}, f32[1]{0:T(128)}, s32[]{:T(128)}, f32[4,1]{0,1:T(1,128)S(1)}, f32[4,1]{0,1:T(1,128)S(1)}, /*index=5*/s32[]{:T(128)}) while((s32[]{:T(128)}, f32[1]{0:T(128)}, s32[]{:T(128)}, f32[4,1]{0,1:T(1,128)S(1)}, f32[4,1]{0,1:T(1,128)S(1)}, /*index=5*/s32[]{:T(128)}) %tuple.323), condition=%wide.region_10.11_spmd, body=%wide.region_9.10_spmd.sunk | while | flops 6 | bytes 143 | solution.py:59
  170.9 2.1 add_dynamic-update-slice_fusion.2
  173.0 10.3 %all-reduce.11 = (f32[4]{0:T(128)S(1)}, f32[4]{0:T(128)S(1)}) all-reduce(f32[4]{0:T(128)S(1)} %get-tuple-element.920, f32[4]{0:T(128)S(1)} %add_dynamic-update-slice_fusion.2), channel_id=8, replica_groups=mesh['axial'=4,'radial'=4,'azim'=2] {'axial'}, use_global_device_ids=true, to_apply=%add.7 | all-reduce | flops 8 | bytes 64
  183.5 5.8 %while.87 = (s32[]{:T(128)}, f32[1]{0:T(128)}, s32[]{:T(128)}, f32[4,1]{0,1:T(1,128)S(1)}, f32[4,1]{0,1:T(1,128)S(1)}, /*index=5*/s32[]{:T(128)}) while((s32[]{:T(128)}, f32[1]{0:T(128)}, s32[]{:T(128)}, f32[4,1]{0,1:T(1,128)S(1)}, f32[4,1]{0,1:T(1,128)S(1)}, /*index=5*/s32[]{:T(128)}) %tuple.326), condition=%wide.region_12.13_spmd, body=%wide.region_11.12_spmd.sunk | while | flops 6 | bytes 143 | solution.py:59
  197.2 4.2 collective-permute-done.23
  201.6 2.8 collective-permute-start.24
  206.1 4.0 collective-permute-done.25
  213.2 2.1 collective-permute-start.28
  217.1 4.3 collective-permute-done.29
  221.7 2.8 collective-permute-start.30
  227.6 3.0 collective-permute-done.31
  235.7 2.9 collective-permute-start.34
  240.3 4.3 collective-permute-done.35
  244.9 2.8 collective-permute-start.36
  249.6 4.3 collective-permute-done.37
  261.8 4.3 collective-permute-done.41
  266.4 2.8 collective-permute-start.42
  271.0 4.3 collective-permute-done.43
  283.2 4.3 collective-permute-done.47
  287.7 12.7 %collective-permute-start.48 = (f32[3,18,1,130]{3,2,1,0:T(1,128)S(1)}, f32[3,18,1,130]{3,2,1,0:T(1,128)S(1)}, u32[]{:S(2)}, u32[]{:S(2)}) collective-permute-start(f32[3,18,1,130]{3,2,1,0:T(1,128)S(1)} %pad_maximum_fusion.68), channel_id=1, source_target_pairs={{0,2},{2,4},{4,6},{1,3},{3,5},{5,7},{8,10},{10,12},{12,14},{9,11},... | collective-permute-start | bytes 84248 | tf_op jit(solution)/shard_map/ppermute | solution.py:36
  306.4 4.2 collective-permute-done.52
  314.3 4.0 collective-permute-done.54
  325.1 4.2 collective-permute-done.58
  329.5 2.8 collective-permute-start.59
  333.9 4.0 collective-permute-done.60
  340.0 8.3 %all-reduce.9 = f32[4]{0:T(128)S(1)} all-reduce(f32[4]{0:T(128)S(1)} %add_dynamic-update-slice_fusion.1), channel_id=10, replica_groups=mesh['axial'=4,'radial'=4,'azim'=2] {'axial'}, use_global_device_ids=true, to_apply=%add.9 | all-reduce | flops 4 | bytes 32
  348.4 5.7 %while.88 = (s32[]{:T(128)}, f32[1]{0:T(128)}, s32[]{:T(128)}, f32[4,1]{0,1:T(1,128)S(1)}, f32[4,1]{0,1:T(1,128)S(1)}, /*index=5*/s32[]{:T(128)}) while((s32[]{:T(128)}, f32[1]{0:T(128)}, s32[]{:T(128)}, f32[4,1]{0,1:T(1,128)S(1)}, f32[4,1]{0,1:T(1,128)S(1)}, /*index=5*/s32[]{:T(128)}) %tuple.325), condition=%wide.region_16.17_spmd, body=%wide.region_15.16_spmd.sunk | while | flops 6 | bytes 143 | solution.py:59
  356.7 10.3 %all-reduce.10 = f32[4]{0:T(128)S(1)} all-reduce(f32[4]{0:T(128)S(1)} %add_dynamic-update-slice_fusion), channel_id=11, replica_groups=mesh['axial'=4,'radial'=4,'azim'=2] {'axial'}, use_global_device_ids=true, to_apply=%add.10 | all-reduce | flops 4 | bytes 32
  367.2 5.7 %while.89 = (s32[]{:T(128)}, f32[1]{0:T(128)}, s32[]{:T(128)}, f32[4,1]{0,1:T(1,128)S(1)}, f32[4,1]{0,1:T(1,128)S(1)}, /*index=5*/s32[]{:T(128)}) while((s32[]{:T(128)}, f32[1]{0:T(128)}, s32[]{:T(128)}, f32[4,1]{0,1:T(1,128)S(1)}, f32[4,1]{0,1:T(1,128)S(1)}, /*index=5*/s32[]{:T(128)}) %tuple.324), condition=%wide.region_18.19_spmd, body=%wide.region_17.18_spmd.sunk | while | flops 6 | bytes 143 | solution.py:59
  380.7 4.2 collective-permute-done.64
  385.1 2.8 collective-permute-start.65
  389.5 4.0 collective-permute-done.66
  396.6 2.1 collective-permute-start.69
  400.5 4.3 collective-permute-done.70
  405.1 2.8 collective-permute-start.71
  409.7 4.3 collective-permute-done.72
  419.1 2.9 collective-permute-start.75
  423.7 4.3 collective-permute-done.76
  428.3 2.8 collective-permute-start.77
  432.9 4.3 collective-permute-done.78
  446.8 4.3 collective-permute-done.82
  451.4 2.8 collective-permute-start.83
  456.0 4.3 collective-permute-done.84
  (367 shorter events, 169.9 us)
Async XLA Ops:
  21.5 21.1 %collective-permute-start.1 = (f32[3,16,1,128]{3,2,1,0:T(1,128)S(1)}, f32[3,16,1,128]{3,2,1,0:T(1,128)S(1)}, u32[]{:S(2)}, u32[]{:S(2)}) collective-permute-start(f32[3,16,1,128]{3,2,1,0:T(1,128)S(1)} %fusion.143), channel_id=1, source_target_pairs={{0,2},{2,4},{4,6},{1,3},{3,5},{5,7},{8,10},{10,12},{12,14},{9,11},... | collective-permute-start | bytes 73736 | tf_op jit(solution)/shard_map/ppermute | solution.py:20
  26.3 14.6 %collective-permute-start = (f32[3,1,16,128]{3,2,1,0:T(8,128)S(1)}, f32[3,1,16,128]{3,2,1,0:T(8,128)S(1)}, u32[]{:S(2)}, u32[]{:S(2)}) collective-permute-start(f32[3,1,16,128]{3,2,1,0:T(8,128)S(1)} %fusion.144), channel_id=1, source_target_pairs={{0,8},{8,16},{16,24},{1,9},{9,17},{17,25},{2,10},{10,18},{18,26},{... | collective-permute-start | bytes 73736 | tf_op jit(solution)/shard_map/ppermute | solution.py:20
  30.7 19.2 %collective-permute-start.2 = (f32[3,16,16,1]{3,2,1,0:T(8,128)}, f32[3,16,16,1]{3,2,1,0:T(8,128)}, u32[]{:S(2)}, u32[]{:S(2)}) collective-permute-start(f32[3,16,16,1]{3,2,1,0:T(8,128)} %fusion.68), channel_id=1, source_target_pairs={{0,1},{1,0},{2,3},{3,2},{4,5},{5,4},{6,7},{7,6},{8,9},{9,8},{10,11... | collective-permute-start | bytes 9224 | tf_op jit(solution)/shard_map/ppermute | solution.py:25
  31.8 3.3 collective-permute-start.3
  32.3 2.8 collective-permute-start.4
  36.1 24.6 %collective-permute-start.5 = (f32[3,1,16,130]{3,2,1,0:T(8,128)S(1)}, f32[3,1,16,130]{3,2,1,0:T(8,128)S(1)}, u32[]{:S(2)}, u32[]{:S(2)}) collective-permute-start(f32[3,1,16,130]{3,2,1,0:T(8,128)S(1)} %get-tuple-element.805), channel_id=1, source_target_pairs={{0,8},{8,16},{16,24},{1,9},{9,17},{17,25},{2,10},{10,18},{18,26},{... | collective-permute-start | bytes 74888 | tf_op jit(solution)/shard_map/ppermute | solution.py:36
  39.6 21.1 %collective-permute-start.6 = (f32[3,1,16,130]{3,2,1,0:T(8,128)S(1)}, f32[3,1,16,130]{3,2,1,0:T(8,128)S(1)}, u32[]{:S(2)}, u32[]{:S(2)}) collective-permute-start(f32[3,1,16,130]{3,2,1,0:T(8,128)S(1)} %get-tuple-element.806), channel_id=1, source_target_pairs={{8,0},{16,8},{24,16},{9,1},{17,9},{25,17},{10,2},{18,10},{26,18},{... | collective-permute-start | bytes 74888 | tf_op jit(solution)/shard_map/ppermute | solution.py:38
  62.3 5.2 %collective-permute-start.7 = (f32[3,18,1,130]{3,2,1,0:T(1,128)S(1)}, f32[3,18,1,130]{3,2,1,0:T(1,128)S(1)}, u32[]{:S(2)}, u32[]{:S(2)}) collective-permute-start(f32[3,18,1,130]{3,2,1,0:T(1,128)S(1)} %pad_maximum_fusion.87), channel_id=1, source_target_pairs={{0,2},{2,4},{4,6},{1,3},{3,5},{5,7},{8,10},{10,12},{12,14},{9,11},... | collective-permute-start | bytes 84248 | tf_op jit(solution)/shard_map/ppermute | solution.py:36
  69.7 2.6 collective-permute-start.8
  69.8 2.5 collective-permute-start.9
  72.3 9.0 %collective-permute-start.10 = (f32[1,16,130]{2,1,0:T(8,128)S(1)}, f32[1,16,130]{2,1,0:T(8,128)S(1)}, u32[]{:S(2)}, u32[]{:S(2)}) collective-permute-start(f32[1,16,130]{2,1,0:T(8,128)S(1)} %get-tuple-element.901), channel_id=1, source_target_pairs={{0,8},{8,16},{16,24},{1,9},{9,17},{17,25},{2,10},{10,18},{18,26},{... | collective-permute-start | bytes 24968 | tf_op jit(solution)/shard_map/ppermute | solution.py:36
  76.9 5.6 %collective-permute-start.11 = (f32[1,16,130]{2,1,0:T(8,128)S(1)}, f32[1,16,130]{2,1,0:T(8,128)S(1)}, u32[]{:S(2)}, u32[]{:S(2)}) collective-permute-start(f32[1,16,130]{2,1,0:T(8,128)S(1)} %get-tuple-element.902), channel_id=1, source_target_pairs={{8,0},{16,8},{24,16},{9,1},{17,9},{25,17},{10,2},{18,10},{26,18},{... | collective-permute-start | bytes 24968 | tf_op jit(solution)/shard_map/ppermute | solution.py:38
  82.7 23.9 %collective-permute-start.12 = (f32[18,1,130]{2,1,0:T(1,128)S(1)}, f32[18,1,130]{2,1,0:T(1,128)S(1)}, u32[]{:S(2)}, u32[]{:S(2)}) collective-permute-start(f32[18,1,130]{2,1,0:T(1,128)S(1)} %get-tuple-element.858), channel_id=1, source_target_pairs={{0,2},{2,4},{4,6},{1,3},{3,5},{5,7},{8,10},{10,12},{12,14},{9,11},... | collective-permute-start | bytes 28088 | tf_op jit(solution)/shard_map/ppermute | solution.py:36
  105.2 6.0 %collective-permute-start.13 = (f32[18,1,130]{2,1,0:T(1,128)S(1)}, f32[18,1,130]{2,1,0:T(1,128)S(1)}, u32[]{:S(2)}, u32[]{:S(2)}) collective-permute-start(f32[18,1,130]{2,1,0:T(1,128)S(1)} %get-tuple-element.857), channel_id=1, source_target_pairs={{2,0},{4,2},{6,4},{3,1},{5,3},{7,5},{10,8},{12,10},{14,12},{11,9},... | collective-permute-start | bytes 28088 | tf_op jit(solution)/shard_map/ppermute | solution.py:38
  112.2 19.4 %collective-permute-start.14 = (f32[16,16,1]{2,1,0:T(8,128)S(1)}, f32[16,16,1]{2,1,0:T(8,128)S(1)}, u32[]{:S(2)}, u32[]{:S(2)}) collective-permute-start(f32[16,16,1]{2,1,0:T(8,128)S(1)} %get-tuple-element.913), channel_id=1, source_target_pairs={{0,1},{1,0},{2,3},{3,2},{4,5},{5,4},{6,7},{7,6},{8,9},{9,8},{10,11... | collective-permute-start | bytes 3080 | tf_op jit(solution)/shard_map/ppermute | solution.py:36
  112.3 19.4 %collective-permute-start.15 = (f32[16,16,1]{2,1,0:T(8,128)S(1)}, f32[16,16,1]{2,1,0:T(8,128)S(1)}, u32[]{:S(2)}, u32[]{:S(2)}) collective-permute-start(f32[16,16,1]{2,1,0:T(8,128)S(1)} %get-tuple-element.914), channel_id=1, source_target_pairs={{1,0},{0,1},{3,2},{2,3},{5,4},{4,5},{7,6},{6,7},{9,8},{8,9},{11,10... | collective-permute-start | bytes 3080 | tf_op jit(solution)/shard_map/ppermute | solution.py:38
  131.7 4.6 collective-permute-start.16
  133.8 5.6 %collective-permute-start.17 = (f32[1,16,130]{2,1,0:T(8,128)S(1)}, f32[1,16,130]{2,1,0:T(8,128)S(1)}, u32[]{:S(2)}, u32[]{:S(2)}) collective-permute-start(f32[1,16,130]{2,1,0:T(8,128)S(1)} %get-tuple-element.900), channel_id=1, source_target_pairs={{8,0},{16,8},{24,16},{9,1},{17,9},{25,17},{10,2},{18,10},{26,18},{... | collective-permute-start | bytes 24968 | tf_op jit(solution)/shard_map/ppermute | solution.py:38
  139.6 7.5 %collective-permute-start.18 = (f32[18,1,130]{2,1,0:T(1,128)S(1)}, f32[18,1,130]{2,1,0:T(1,128)S(1)}, u32[]{:S(2)}, u32[]{:S(2)}) collective-permute-start(f32[18,1,130]{2,1,0:T(1,128)S(1)} %get-tuple-element.856), channel_id=1, source_target_pairs={{0,2},{2,4},{4,6},{1,3},{3,5},{5,7},{8,10},{10,12},{12,14},{9,11},... | collective-permute-start | bytes 28088 | tf_op jit(solution)/shard_map/ppermute | solution.py:36
  145.8 5.6 %collective-permute-start.19 = (f32[18,1,130]{2,1,0:T(1,128)S(1)}, f32[18,1,130]{2,1,0:T(1,128)S(1)}, u32[]{:S(2)}, u32[]{:S(2)}) collective-permute-start(f32[18,1,130]{2,1,0:T(1,128)S(1)} %get-tuple-element.855), channel_id=1, source_target_pairs={{2,0},{4,2},{6,4},{3,1},{5,3},{7,5},{10,8},{12,10},{14,12},{11,9},... | collective-permute-start | bytes 28088 | tf_op jit(solution)/shard_map/ppermute | solution.py:38
  193.9 3.3 collective-permute-start.22
  195.8 5.6 %collective-permute-start.23 = (f32[1,16,130]{2,1,0:T(8,128)S(1)}, f32[1,16,130]{2,1,0:T(8,128)S(1)}, u32[]{:S(2)}, u32[]{:S(2)}) collective-permute-start(f32[1,16,130]{2,1,0:T(8,128)S(1)} %get-tuple-element.898), channel_id=1, source_target_pairs={{8,0},{16,8},{24,16},{9,1},{17,9},{25,17},{10,2},{18,10},{26,18},{... | collective-permute-start | bytes 24968 | tf_op jit(solution)/shard_map/ppermute | solution.py:38
  201.6 4.3 collective-permute-start.24
  204.4 5.7 %collective-permute-start.25 = (f32[18,1,130]{2,1,0:T(1,128)S(1)}, f32[18,1,130]{2,1,0:T(1,128)S(1)}, u32[]{:S(2)}, u32[]{:S(2)}) collective-permute-start(f32[18,1,130]{2,1,0:T(1,128)S(1)} %get-tuple-element.853), channel_id=1, source_target_pairs={{2,0},{4,2},{6,4},{3,1},{5,3},{7,5},{10,8},{12,10},{14,12},{11,9},... | collective-permute-start | bytes 28088 | tf_op jit(solution)/shard_map/ppermute | solution.py:38
  213.2 3.9 collective-permute-start.28
  215.3 6.0 %collective-permute-start.29 = (f32[3,1,16,130]{3,2,1,0:T(8,128)S(1)}, f32[3,1,16,130]{3,2,1,0:T(8,128)S(1)}, u32[]{:S(2)}, u32[]{:S(2)}) collective-permute-start(f32[3,1,16,130]{3,2,1,0:T(8,128)S(1)} %get-tuple-element.804), channel_id=1, source_target_pairs={{8,0},{16,8},{24,16},{9,1},{17,9},{25,17},{10,2},{18,10},{26,18},{... | collective-permute-start | bytes 74888 | tf_op jit(solution)/shard_map/ppermute | solution.py:38
  221.7 5.8 %collective-permute-start.30 = (f32[3,18,1,130]{3,2,1,0:T(1,128)S(1)}, f32[3,18,1,130]{3,2,1,0:T(1,128)S(1)}, u32[]{:S(2)}, u32[]{:S(2)}) collective-permute-start(f32[3,18,1,130]{3,2,1,0:T(1,128)S(1)} %get-tuple-element.777), channel_id=1, source_target_pairs={{0,2},{2,4},{4,6},{1,3},{3,5},{5,7},{8,10},{10,12},{12,14},{9,11},... | collective-permute-start | bytes 84248 | tf_op jit(solution)/shard_map/ppermute | solution.py:36
  224.5 6.0 %collective-permute-start.31 = (f32[3,18,1,130]{3,2,1,0:T(1,128)S(1)}, f32[3,18,1,130]{3,2,1,0:T(1,128)S(1)}, u32[]{:S(2)}, u32[]{:S(2)}) collective-permute-start(f32[3,18,1,130]{3,2,1,0:T(1,128)S(1)} %get-tuple-element.778), channel_id=1, source_target_pairs={{2,0},{4,2},{6,4},{3,1},{5,3},{7,5},{10,8},{12,10},{14,12},{11,9},... | collective-permute-start | bytes 84248 | tf_op jit(solution)/shard_map/ppermute | solution.py:38
  235.7 4.6 collective-permute-start.34
  238.6 6.0 %collective-permute-start.35 = (f32[3,1,16,130]{3,2,1,0:T(8,128)S(1)}, f32[3,1,16,130]{3,2,1,0:T(8,128)S(1)}, u32[]{:S(2)}, u32[]{:S(2)}) collective-permute-start(f32[3,1,16,130]{3,2,1,0:T(8,128)S(1)} %get-tuple-element.802), channel_id=1, source_target_pairs={{8,0},{16,8},{24,16},{9,1},{17,9},{25,17},{10,2},{18,10},{26,18},{... | collective-permute-start | bytes 74888 | tf_op jit(solution)/shard_map/ppermute | solution.py:38
  244.9 4.6 collective-permute-start.36
  247.8 6.0 %collective-permute-start.37 = (f32[3,18,1,130]{3,2,1,0:T(1,128)S(1)}, f32[3,18,1,130]{3,2,1,0:T(1,128)S(1)}, u32[]{:S(2)}, u32[]{:S(2)}) collective-permute-start(f32[3,18,1,130]{3,2,1,0:T(1,128)S(1)} %get-tuple-element.776), channel_id=1, source_target_pairs={{2,0},{4,2},{6,4},{3,1},{5,3},{7,5},{10,8},{12,10},{14,12},{11,9},... | collective-permute-start | bytes 84248 | tf_op jit(solution)/shard_map/ppermute | solution.py:38
  255.7 2.3 collective-permute-start.39
  258.1 3.7 collective-permute-start.40
  260.0 6.0 %collective-permute-start.41 = (f32[3,1,16,130]{3,2,1,0:T(8,128)S(1)}, f32[3,1,16,130]{3,2,1,0:T(8,128)S(1)}, u32[]{:S(2)}, u32[]{:S(2)}) collective-permute-start(f32[3,1,16,130]{3,2,1,0:T(8,128)S(1)} %get-tuple-element.800), channel_id=1, source_target_pairs={{8,0},{16,8},{24,16},{9,1},{17,9},{25,17},{10,2},{18,10},{26,18},{... | collective-permute-start | bytes 74888 | tf_op jit(solution)/shard_map/ppermute | solution.py:38
  266.4 4.6 collective-permute-start.42
  269.2 6.0 %collective-permute-start.43 = (f32[3,18,1,130]{3,2,1,0:T(1,128)S(1)}, f32[3,18,1,130]{3,2,1,0:T(1,128)S(1)}, u32[]{:S(2)}, u32[]{:S(2)}) collective-permute-start(f32[3,18,1,130]{3,2,1,0:T(1,128)S(1)} %get-tuple-element.774), channel_id=1, source_target_pairs={{2,0},{4,2},{6,4},{3,1},{5,3},{7,5},{10,8},{12,10},{14,12},{11,9},... | collective-permute-start | bytes 84248 | tf_op jit(solution)/shard_map/ppermute | solution.py:38
  279.5 3.7 collective-permute-start.46
  281.5 6.0 %collective-permute-start.47 = (f32[3,1,16,130]{3,2,1,0:T(8,128)S(1)}, f32[3,1,16,130]{3,2,1,0:T(8,128)S(1)}, u32[]{:S(2)}, u32[]{:S(2)}) collective-permute-start(f32[3,1,16,130]{3,2,1,0:T(8,128)S(1)} %get-tuple-element.798), channel_id=1, source_target_pairs={{8,0},{16,8},{24,16},{9,1},{17,9},{25,17},{10,2},{18,10},{26,18},{... | collective-permute-start | bytes 74888 | tf_op jit(solution)/shard_map/ppermute | solution.py:38
  287.7 12.7 %collective-permute-start.48 = (f32[3,18,1,130]{3,2,1,0:T(1,128)S(1)}, f32[3,18,1,130]{3,2,1,0:T(1,128)S(1)}, u32[]{:S(2)}, u32[]{:S(2)}) collective-permute-start(f32[3,18,1,130]{3,2,1,0:T(1,128)S(1)} %pad_maximum_fusion.68), channel_id=1, source_target_pairs={{0,2},{2,4},{4,6},{1,3},{3,5},{5,7},{8,10},{10,12},{12,14},{9,11},... | collective-permute-start | bytes 84248 | tf_op jit(solution)/shard_map/ppermute | solution.py:36
  303.0 3.4 collective-permute-start.51
  304.9 5.6 %collective-permute-start.52 = (f32[1,16,130]{2,1,0:T(8,128)S(1)}, f32[1,16,130]{2,1,0:T(8,128)S(1)}, u32[]{:S(2)}, u32[]{:S(2)}) collective-permute-start(f32[1,16,130]{2,1,0:T(8,128)S(1)} %get-tuple-element.888), channel_id=1, source_target_pairs={{8,0},{16,8},{24,16},{9,1},{17,9},{25,17},{10,2},{18,10},{26,18},{... | collective-permute-start | bytes 24968 | tf_op jit(solution)/shard_map/ppermute | solution.py:38
  310.7 3.4 collective-permute-start.53
  312.7 5.7 %collective-permute-start.54 = (f32[18,1,130]{2,1,0:T(1,128)S(1)}, f32[18,1,130]{2,1,0:T(1,128)S(1)}, u32[]{:S(2)}, u32[]{:S(2)}) collective-permute-start(f32[18,1,130]{2,1,0:T(1,128)S(1)} %get-tuple-element.851), channel_id=1, source_target_pairs={{2,0},{4,2},{6,4},{3,1},{5,3},{7,5},{10,8},{12,10},{14,12},{11,9},... | collective-permute-start | bytes 28088 | tf_op jit(solution)/shard_map/ppermute | solution.py:38
  321.7 3.4 collective-permute-start.57
  323.6 5.6 %collective-permute-start.58 = (f32[1,16,130]{2,1,0:T(8,128)S(1)}, f32[1,16,130]{2,1,0:T(8,128)S(1)}, u32[]{:S(2)}, u32[]{:S(2)}) collective-permute-start(f32[1,16,130]{2,1,0:T(8,128)S(1)} %get-tuple-element.886), channel_id=1, source_target_pairs={{8,0},{16,8},{24,16},{9,1},{17,9},{25,17},{10,2},{18,10},{26,18},{... | collective-permute-start | bytes 24968 | tf_op jit(solution)/shard_map/ppermute | solution.py:38
  329.5 4.3 collective-permute-start.59
  332.3 5.7 %collective-permute-start.60 = (f32[18,1,130]{2,1,0:T(1,128)S(1)}, f32[18,1,130]{2,1,0:T(1,128)S(1)}, u32[]{:S(2)}, u32[]{:S(2)}) collective-permute-start(f32[18,1,130]{2,1,0:T(1,128)S(1)} %get-tuple-element.849), channel_id=1, source_target_pairs={{2,0},{4,2},{6,4},{3,1},{5,3},{7,5},{10,8},{12,10},{14,12},{11,9},... | collective-permute-start | bytes 28088 | tf_op jit(solution)/shard_map/ppermute | solution.py:38
  377.4 3.3 collective-permute-start.63
  379.2 5.6 %collective-permute-start.64 = (f32[1,16,130]{2,1,0:T(8,128)S(1)}, f32[1,16,130]{2,1,0:T(8,128)S(1)}, u32[]{:S(2)}, u32[]{:S(2)}) collective-permute-start(f32[1,16,130]{2,1,0:T(8,128)S(1)} %get-tuple-element.884), channel_id=1, source_target_pairs={{8,0},{16,8},{24,16},{9,1},{17,9},{25,17},{10,2},{18,10},{26,18},{... | collective-permute-start | bytes 24968 | tf_op jit(solution)/shard_map/ppermute | solution.py:38
  385.1 4.3 collective-permute-start.65
  387.9 5.7 %collective-permute-start.66 = (f32[18,1,130]{2,1,0:T(1,128)S(1)}, f32[18,1,130]{2,1,0:T(1,128)S(1)}, u32[]{:S(2)}, u32[]{:S(2)}) collective-permute-start(f32[18,1,130]{2,1,0:T(1,128)S(1)} %get-tuple-element.847), channel_id=1, source_target_pairs={{2,0},{4,2},{6,4},{3,1},{5,3},{7,5},{10,8},{12,10},{14,12},{11,9},... | collective-permute-start | bytes 28088 | tf_op jit(solution)/shard_map/ppermute | solution.py:38
  396.6 3.9 collective-permute-start.69
  398.8 6.0 %collective-permute-start.70 = (f32[3,1,16,130]{3,2,1,0:T(8,128)S(1)}, f32[3,1,16,130]{3,2,1,0:T(8,128)S(1)}, u32[]{:S(2)}, u32[]{:S(2)}) collective-permute-start(f32[3,1,16,130]{3,2,1,0:T(8,128)S(1)} %get-tuple-element.796), channel_id=1, source_target_pairs={{8,0},{16,8},{24,16},{9,1},{17,9},{25,17},{10,2},{18,10},{26,18},{... | collective-permute-start | bytes 74888 | tf_op jit(solution)/shard_map/ppermute | solution.py:38
  405.1 4.6 collective-permute-start.71
  408.0 6.0 %collective-permute-start.72 = (f32[3,18,1,130]{3,2,1,0:T(1,128)S(1)}, f32[3,18,1,130]{3,2,1,0:T(1,128)S(1)}, u32[]{:S(2)}, u32[]{:S(2)}) collective-permute-start(f32[3,18,1,130]{3,2,1,0:T(1,128)S(1)} %get-tuple-element.772), channel_id=1, source_target_pairs={{2,0},{4,2},{6,4},{3,1},{5,3},{7,5},{10,8},{12,10},{14,12},{11,9},... | collective-permute-start | bytes 84248 | tf_op jit(solution)/shard_map/ppermute | solution.py:38
  419.1 4.6 collective-permute-start.75
  421.9 6.0 %collective-permute-start.76 = (f32[3,1,16,130]{3,2,1,0:T(8,128)S(1)}, f32[3,1,16,130]{3,2,1,0:T(8,128)S(1)}, u32[]{:S(2)}, u32[]{:S(2)}) collective-permute-start(f32[3,1,16,130]{3,2,1,0:T(8,128)S(1)} %get-tuple-element.794), channel_id=1, source_target_pairs={{8,0},{16,8},{24,16},{9,1},{17,9},{25,17},{10,2},{18,10},{26,18},{... | collective-permute-start | bytes 74888 | tf_op jit(solution)/shard_map/ppermute | solution.py:38
  428.3 4.6 collective-permute-start.77
  431.1 6.0 %collective-permute-start.78 = (f32[3,18,1,130]{3,2,1,0:T(1,128)S(1)}, f32[3,18,1,130]{3,2,1,0:T(1,128)S(1)}, u32[]{:S(2)}, u32[]{:S(2)}) collective-permute-start(f32[3,18,1,130]{3,2,1,0:T(1,128)S(1)} %get-tuple-element.770), channel_id=1, source_target_pairs={{2,0},{4,2},{6,4},{3,1},{5,3},{7,5},{10,8},{12,10},{14,12},{11,9},... | collective-permute-start | bytes 84248 | tf_op jit(solution)/shard_map/ppermute | solution.py:38
  443.1 3.7 collective-permute-start.81
  445.1 6.0 %collective-permute-start.82 = (f32[3,1,16,130]{3,2,1,0:T(8,128)S(1)}, f32[3,1,16,130]{3,2,1,0:T(8,128)S(1)}, u32[]{:S(2)}, u32[]{:S(2)}) collective-permute-start(f32[3,1,16,130]{3,2,1,0:T(8,128)S(1)} %get-tuple-element.792), channel_id=1, source_target_pairs={{8,0},{16,8},{24,16},{9,1},{17,9},{25,17},{10,2},{18,10},{26,18},{... | collective-permute-start | bytes 74888 | tf_op jit(solution)/shard_map/ppermute | solution.py:38
  451.4 4.6 collective-permute-start.83
  454.2 6.0 %collective-permute-start.84 = (f32[3,18,1,130]{3,2,1,0:T(1,128)S(1)}, f32[3,18,1,130]{3,2,1,0:T(1,128)S(1)}, u32[]{:S(2)}, u32[]{:S(2)}) collective-permute-start(f32[3,18,1,130]{3,2,1,0:T(1,128)S(1)} %get-tuple-element.768), channel_id=1, source_target_pairs={{2,0},{4,2},{6,4},{3,1},{5,3},{7,5},{10,8},{12,10},{14,12},{11,9},... | collective-permute-start | bytes 84248 | tf_op jit(solution)/shard_map/ppermute | solution.py:38
  (37 other events, 420.3 us)
where the time goes:
time: 472 us; the launch traced here: 463 us
  starting transfers between devices  136 us (29%)
  waiting for transfers between devices  124 us (26%)
  other arithmetic  56.2 us (12%)
  blocking collectives  47.6 us (10%)
  local copies, waits for them, and re-layouts  43.4 us (9%)
  loops' own time  30.1 us (6%)
  matrix products  18.6 us (4%)
  between operations  7.21 us (2%)
    ppermute x40, waiting for transfers between devices, with_halo(): lax.ppermute(head, axis, [((i + 1) % count, i) for i in range(ends)])  104 us
    ppermute x42, starting transfers between devices, with_halo(): lax.ppermute(tail, axis, [(i, (i + 1) % count) for i in range(ends)])  87.4 us
    unnamed x5, blocking collectives  47.6 us
    ppermute x40, starting transfers between devices, with_halo(): lax.ppermute(head, axis, [((i + 1) % count, i) for i in range(ends)])  40 us
    another operation x5, loops' own time, prefix(): return lax.fori_loop(0, count - 1, turn, running)  30 us
    ppermute x42, waiting for transfers between devices, with_halo(): lax.ppermute(tail, axis, [(i, (i + 1) % count) for i in range(ends)])  19.5 us
    dot_general x16, matrix products, lookup(): jnp.dot(tables, onehot, precision=lax.Precision.HIGHEST, preferred_elemen...  18.6 us
    unnamed x9, other arithmetic  17.9 us
  transfers between devices with their start and end apart: 85, of which 68 were waited for; matrix products, arithmetic and copies ran while one was open for 10% of the time, Pallas kernels for 0%

commit v1 on v0

v1 whole, which is shorter than its diff:
```python
import functools

import jax
import jax.numpy as jnp
from jax import lax
from jax.experimental import pallas as pl
from jax.experimental.pallas import tpu as pltpu
from jax.sharding import PartitionSpec as P

BA = 8
CYCLES = 2
NS = 2
ES = 2
HALO = 4
MESH = pl.DeviceIdType.MESH

relax_edge = 0.4
relax_node = 0.6
ground_share = 0.01

NEIGHBOURS = [(0, -1), (0, 1), (-1, 0), (1, 0), (-1, -1), (-1, 1), (1, -1), (1, 1)]


def kernel(groups, radials, source, region, flags, table, out_sol, out_res,
           pack, swap_in, main, inv, ninv, nres, chg, pot, sol, stage, fin,
           tot_out, tot_in, ysolve, pivs, ends,
           ax0, rs0, rr0, cs0, cr0, ax1, rs1, rr1, cs1, cr1,
           pa0, ps0, pr0, pcs0, pcr0, pa1, ps1, pr1, pcs1, pcr1,
           swap_sems, ex_send, ex_recv, tot_send, tot_recv):
    ax = lax.axis_index("axial")
    rd = lax.axis_index("radial")
    core = lax.axis_index("azim")
    mine = 2 * ax + core
    rows = source.shape[2]
    lanes = source.shape[3]
    frame_rows = main.shape[2]
    wide = main.shape[3]
    first, last = HALO, HALO + BA

    def device(group, radial):
        return {"axial": group // 2, "radial": radial, "azim": lax.rem(group, 2)}

    def when_radial(step):
        if step == 0:
            return lambda f: f()
        ok = rd > 0 if step < 0 else rd < radials - 1
        return pl.when(ok)

    def exists(da, dr):
        ok = None
        if da:
            ok = mine > 0 if da < 0 else mine < groups - 1
        if dr:
            ok_r = rd > 0 if dr < 0 else rd < radials - 1
            ok = ok_r if ok is None else jnp.logical_and(ok, ok_r)
        return ok

    barrier = pltpu.get_barrier_semaphore()

    def each_peer(act):
        for dr in (-1, 0, 1):
            def block(dr=dr):
                for k in range(0 if dr else 1, groups):
                    act(dr, k)
            when_radial(dr)(block)

    def greet(dr, k):
        pl.semaphore_signal(barrier, inc=1, device_id=device(lax.rem(mine + k, groups), rd + dr),
                            device_id_type=MESH)

    each_peer(greet)

    pieces = table.shape[0] // 2
    own_layers = source.shape[1]

    def look(layer, carry):
        free = (1 - flags[layer]).astype(jnp.float32)
        for comp in range(3):
            pack[comp, layer] = free * source[comp, layer]
        for top in range(0, rows, 8):
            ids = region[layer, top:top + 8, :]
            low = jnp.bitwise_and(ids, 127)
            high = lax.shift_right_logical(ids, 7)
            for which in range(2):
                value = jnp.zeros((8, lanes), jnp.float32)
                for piece in range(pieces):
                    row = which * pieces + piece
                    line = jnp.broadcast_to(table[row:row + 1, :], (8, 128))
                    got = jnp.take_along_axis(line, low, axis=1, mode="promise_in_bounds")
                    value = jnp.where(high == piece, got, value)
                pack[3 + which, layer, top:top + 8, :] = value
        pack[5, layer] = free
        return carry

    lax.fori_loop(0, own_layers, look, 0)

    columns = 1 + (rd > 0).astype(jnp.int32) + (rd < radials - 1).astype(jnp.int32)
    pl.semaphore_wait(barrier, columns * groups - 1)

    other = 1 - core
    swap = pltpu.make_async_remote_copy(
        src_ref=pack.at[:, pl.ds(other * BA, BA)], dst_ref=swap_in,
        send_sem=swap_sems.at[0], recv_sem=swap_sems.at[1],
        device_id={"axial": ax, "radial": rd, "azim": other}, device_id_type=MESH)
    swap.start()
    swap.wait()
    is_low = core == 0

    def place(layer, carry):
        for field in range(6):
            here = pack[field, core * BA + layer]
            there = swap_in[field, layer]
            main[field, first + layer, 0:rows, 0:lanes] = jnp.where(is_low, here, there)
            main[field, first + layer, 0:rows, lanes:wide] = jnp.where(is_low, there, here)
        return carry

    lax.fori_loop(0, BA, place, 0)

    sub = lax.broadcasted_iota(jnp.int32, (8, wide), 0)
    low_half = sub < 4

    def turn(value):
        return pltpu.roll(value, 4, axis=0)

    def swap_rows(fields, buf, count, depth, base):
        axial, rsend, rrecv, csend, crecv = buf
        copies = []

        def send(index, da, dr, src, dst):
            copy = pltpu.make_async_remote_copy(
                src_ref=src, dst_ref=dst,
                send_sem=ex_send.at[base + index], recv_sem=ex_recv.at[base + index],
                device_id=device(mine + da, rd + dr), device_id_type=MESH)
            ok = exists(da, dr)
            back = exists(-da, -dr)
            pl.when(ok)(lambda: copy.start())
            copies.append((ok, back, copy))

        send(0, 1, 0, fields.at[0:count, last - depth:last, 0:rows, :], axial.at[0])
        send(1, -1, 0, fields.at[0:count, first:first + depth, 0:rows, :], axial.at[1])

        def pack_rows(dst, layer_lo, half, dr):
            top = rows - 8 if dr > 0 else 0

            def body(pair, carry):
                for field in range(count):
                    a = fields[field, layer_lo + pair, top:top + 8, :]
                    b = fields[field, layer_lo + half + pair, top:top + 8, :]
                    if dr > 0:
                        dst[field, pair] = jnp.where(low_half, turn(b), a)
                    else:
                        dst[field, pair] = jnp.where(low_half, a, turn(b))
                return carry

            lax.fori_loop(0, half, body, 0)

        for index, dr in ((0, 1), (1, -1)):
            pack_rows(rsend.at[index], first, BA // 2, dr)
            send(2 + index, 0, dr, rsend.at[index], rrecv.at[index])
        slot = 0
        for da in (1, -1):
            for dr in (1, -1):
                lo = last - HALO if da > 0 else first
                pack_rows(csend.at[slot], lo, HALO // 2, dr)
                send(4 + slot, da, dr, csend.at[slot], crecv.at[slot])
                slot += 1

        def finish():
            for ok, back, copy in copies:
                pl.when(ok)(lambda copy=copy: copy.wait_send())
                pl.when(back)(lambda copy=copy: copy.wait_recv())
            for index, da in ((0, -1), (1, 1)):
                ok = exists(da, 0)

                def body(layer, carry, index=index, da=da, ok=ok):
                    to = layer + (first - depth if da < 0 else last)
                    for field in range(count):
                        fields[field, to, 0:rows, :] = jnp.where(ok, axial[index, field, layer], 0.0)
                    return carry

                lax.fori_loop(0, depth, body, 0)

            def unpack(from_low, from_up, low_ok, up_ok, layer_lo, half):
                def body(pair, carry):
                    for field in range(count):
                        down = jnp.where(low_ok, from_low[field, pair], 0.0)
                        up = jnp.where(up_ok, from_up[field, pair], 0.0)
                        fields[field, layer_lo + pair, rows:frame_rows, :] = jnp.where(low_half, up, down)
                        fields[field, layer_lo + half + pair, rows:frame_rows, :] = turn(
                            jnp.where(low_half, down, up))
                    return carry

                lax.fori_loop(0, half, body, 0)

            unpack(rrecv.at[0], rrecv.at[1], exists(0, -1), exists(0, 1), first, BA // 2)
            unpack(crecv.at[0], crecv.at[1], exists(-1, -1), exists(-1, 1), first - HALO, HALO // 2)
            unpack(crecv.at[2], crecv.at[3], exists(1, -1), exists(1, 1), last, HALO // 2)

        return finish

    def share(which):
        copies = []

        def build(dr, k):
            peer = lax.rem(mine + k, groups)
            copy = pltpu.make_async_remote_copy(
                src_ref=tot_out.at[which], dst_ref=tot_in.at[which, 1 - dr, mine],
                send_sem=tot_send.at[which, dr + 1, k], recv_sem=tot_recv.at[which, 1 - dr, mine],
                device_id=device(peer, rd + dr), device_id_type=MESH)
            copy.start()

        each_peer(build)
        tot_in[which, 1, mine] = tot_out[which]

        def finish():
            def done(dr, k):
                peer = lax.rem(mine + k, groups)
                copy = pltpu.make_async_remote_copy(
                    src_ref=tot_out.at[which], dst_ref=tot_in.at[which, 1 + dr, peer],
                    send_sem=tot_send.at[which, dr + 1, k], recv_sem=tot_recv.at[which, 1 + dr, peer],
                    device_id=device(peer, rd + dr), device_id_type=MESH)
                copy.wait_send()
                copy.wait_recv()

            each_peer(done)

        return finish

    tile_row = lax.broadcasted_iota(jnp.int32, (8, 128), 0)
    odd = jnp.bitwise_and(tile_row, 1) == 1
    has_low, has_up = exists(0, -1), exists(0, 1)

    def column(which, group, row=0):
        low = jnp.where(has_low, tot_in[which, 0, group, row:row + 8, :], 1.0)
        up = jnp.where(has_up, tot_in[which, 2, group, row:row + 8, :], 1.0)
        here = tot_in[which, 1, group, row:row + 8, :]
        return jnp.where(tile_row < 2, low, jnp.where(tile_row < 4, here, up))

    def halves(value):
        left = jnp.sum(value[:, 0:lanes], keepdims=True)
        right = jnp.sum(value[:, lanes:wide], keepdims=True)
        return jnp.where(odd, jnp.broadcast_to(right, (8, 128)), jnp.broadcast_to(left, (8, 128)))

    bufs_main = (ax0, rs0, rr0, cs0, cr0)
    finish_main = swap_rows(main, bufs_main, 6, 3, 0)
    tot_out[0, 0:8] = halves(main[4, last - 1, 0:rows, :])
    tot_out[0, 8:16] = ground_share * halves(main[4, first, 0:rows, :])
    finish_coef = share(0)
    finish_main()

    def back_r(x):
        return pltpu.roll(x, 1, axis=0)

    def back_l(x):
        return pltpu.roll(x, 1, axis=1)

    def fore_r(x):
        return pltpu.roll(x, frame_rows - 1, axis=0)

    def fore_l(x):
        return pltpu.roll(x, wide - 1, axis=1)

    def setup(layer, carry):
        reluct, conduct, free = main[3, layer], main[4, layer], main[5, layer]
        low0, low1, low2 = main[3, layer - 1], back_r(reluct), back_l(reluct)
        base = 2.0 * reluct + conduct + (1.0 - free)
        scaled = relax_edge * free
        inv[0, layer] = scaled / (base + low1 + low2)
        inv[1, layer] = scaled / (base + low0 + low2)
        inv[2, layer] = scaled / (base + low0 + low1)
        nodes = 3.0 * conduct + main[4, layer - 1] + back_r(conduct) + back_l(conduct)
        inside = conduct > 0.0
        ninv[layer] = jnp.where(inside, relax_node / jnp.where(inside, nodes, 1.0), 0.0)
        return carry

    lax.fori_loop(first - 2, last + 2, setup, 0)

    finish_coef()
    previous = None
    coupling = None
    for group in range(groups):
        nxt = column(0, group)
        ground = column(0, group, 8)
        if group == 0:
            pivot = nxt + ground
            slope = jnp.zeros_like(nxt)
        else:
            pivot = coupling + nxt + ground - coupling * coupling / previous
            slope = coupling
        previous, coupling = pivot, nxt
        pivs[0, group] = 1.0 / pivot
        pivs[1, group] = slope / pivot
        pivs[2, group] = nxt / pivot
    ysolve[0] = jnp.zeros((8, 128), jnp.float32)
    ysolve[groups + 1] = jnp.zeros((8, 128), jnp.float32)

    def sweep(lo, hi, edges, first_cycle):
        def fields_of(layer, u0, u1, u2, up1, up2):
            weight = main[3, layer]
            h1 = weight * (fore_l(u0) - u0 - (up2 - u2))
            h2 = weight * ((up1 - u1) - (fore_r(u0) - u0))
            return weight, h1, h2

        def body(layer, carry):
            u0, u1, u2, h1_low, h2_low = carry
            n0, n1, n2 = edges(layer + 1)
            weight, h1, h2 = fields_of(layer, u0, u1, u2, n1, n2)
            h0 = weight * ((fore_r(u2) - u2) - (fore_l(u1) - u1))
            conduct, free = main[4, layer], main[5, layer]
            a0 = (back_l(h1) - h1) - (back_r(h2) - h2) + conduct * u0
            a1 = (h2_low - h2) - (back_l(h0) - h0) + conduct * u1
            a2 = (back_r(h0) - h0) - (h1_low - h1) + conduct * u2
            main[0, layer] = main[0, layer] - free * a0
            main[1, layer] = main[1, layer] - free * a1
            main[2, layer] = main[2, layer] - free * a2

            @pl.when(jnp.logical_and(layer >= first, layer < last))
            def _():
                for comp, u in enumerate((u0, u1, u2)):
                    if first_cycle:
                        sol[comp, layer - first] = u[0:rows]
                    else:
                        sol[comp, layer - first] = sol[comp, layer - first] + u[0:rows]

            return n0, n1, n2, h1, h2

        b0, b1, b2 = edges(lo - 1)
        c0, c1, c2 = edges(lo)
        _, h1, h2 = fields_of(lo - 1, b0, b1, b2, c1, c2)
        lax.fori_loop(lo, hi, body, (c0, c1, c2, h1, h2))

    def corrections(layer):
        p = pot[0, layer]
        free = main[5, layer]
        return free * (pot[0, layer + 1] - p), free * (fore_r(p) - p), free * (fore_l(p) - p)

    def relaxed(layer):
        return inv[0, layer] * main[0, layer], inv[1, layer] * main[1, layer], inv[2, layer] * main[2, layer]

    def laplace(layer, low_flux):
        p = chg[layer]
        weight = main[4, layer] * main[5, layer]
        f0 = weight * (chg[layer + 1] - p)
        f1 = weight * (fore_r(p) - p)
        f2 = weight * (fore_l(p) - p)
        value = (low_flux - f0) + (back_r(f1) - f1) + (back_l(f2) - f2)
        return value, f0

    def low_flux_of(layer):
        return main[4, layer] * main[5, layer] * (chg[layer + 1] - chg[layer])

    for cycle in range(CYCLES):
        if cycle:
            swap_rows(main, (ax1, rs1, rr1, cs1, cr1), 3, 3, 8)()

        def node(layer, carry):
            r0, r1, r2 = main[0, layer], main[1, layer], main[2, layer]
            value = (main[0, layer - 1] - r0) + (back_r(r1) - r1) + (back_l(r2) - r2)
            nres[layer] = value
            chg[layer] = ninv[layer] * value
            return carry

        lax.fori_loop(first - 2, last + 2, node, 0)

        def second(layer, flux):
            value, flux = laplace(layer, flux)
            value = nres[layer] - value
            nres[layer] = value
            pot[0, layer] = chg[layer]
            return flux

        lax.fori_loop(first - 1, last + 1, second, low_flux_of(first - 2))

        def advance(layer, carry):
            change = ninv[layer] * nres[layer]
            chg[layer] = change
            pot[0, layer] = pot[0, layer] + change
            return carry

        lax.fori_loop(first - 1, last + 1, advance, 0)

        bufs_pot = (pa0, ps0, pr0, pcs0, pcr0) if cycle == 0 else (pa1, ps1, pr1, pcs1, pcr1)
        finish_pot = swap_rows(pot, bufs_pot, 1, 4, 16 + 8 * cycle)

        def total(layer, carry):
            flux, acc = carry
            value, flux = laplace(layer, flux)
            return flux, acc + (nres[layer] - value)[0:rows]

        _, acc = lax.fori_loop(first, last, total,
                               (low_flux_of(first - 1), jnp.zeros((rows, wide), jnp.float32)))
        tot_out[1 + cycle, 0:8] = halves(acc)
        tot_out[1 + cycle, 8:16] = jnp.zeros((8, 128), jnp.float32)
        finish_tot = share(1 + cycle)
        finish_pot()
        finish_tot()

        z = jnp.zeros((8, 128), jnp.float32)
        for group in range(groups):
            z = pivs[0, group] * column(1 + cycle, group) + pivs[1, group] * z
            ysolve[1 + group] = z
        y = jnp.zeros((8, 128), jnp.float32)
        for group in reversed(range(groups)):
            y = ysolve[1 + group] + pivs[2, group] * y
            ysolve[1 + group] = y

        def line(tile, low):
            return jnp.concatenate([tile[low:low + 1, :], tile[low + 1:low + 2, :]], axis=1)

        for part, (lo, hi) in enumerate(((0, first), (first, last), (last, last + HALO))):
            tile = ysolve[mine + part]
            here = jnp.broadcast_to(line(tile, 2), (rows, wide))
            up = jnp.broadcast_to(jnp.where(has_up, line(tile, 4), 0.0), (8, wide))
            down = jnp.broadcast_to(jnp.where(has_low, line(tile, 0), 0.0), (8, wide))
            spread = jnp.concatenate([here, jnp.where(low_half, up, down)], axis=0)

            def lift(layer, carry, spread=spread):
                pot[0, layer] = pot[0, layer] + spread
                return carry

            lax.fori_loop(lo, hi, lift, 0)

        sweep(first - 2, last + 2, corrections, cycle == 0)
        sweep(first - 1, last + 1, relaxed, False)
        sweep(first, last, relaxed, False)

    def split(layer, carry):
        for comp in range(3):
            for which in range(2):
                value = sol[comp, layer] if which == 0 else main[comp, first + layer, 0:rows, :]
                left, right = value[:, 0:lanes], value[:, lanes:wide]
                out = out_sol if which == 0 else out_res
                out[comp, core * BA + layer] = jnp.where(is_low, left, right)
                stage[which, comp, layer] = jnp.where(is_low, right, left)
        return carry

    lax.fori_loop(0, BA, split, 0)
    final = pltpu.make_async_remote_copy(
        src_ref=stage, dst_ref=fin, send_sem=swap_sems.at[2], recv_sem=swap_sems.at[3],
        device_id={"axial": ax, "radial": rd, "azim": other}, device_id_type=MESH)
    final.start()
    final.wait()

    def fetch(layer, carry):
        for comp in range(3):
            out_sol[comp, other * BA + layer] = fin[0, comp, layer]
            out_res[comp, other * BA + layer] = fin[1, comp, layer]
        return carry

    lax.fori_loop(0, BA, fetch, 0)


def on_device(groups, radials, source, region, flags, reluctivity_table, conductivity_table):
    _, layers, rows, lanes = source.shape
    f32 = jnp.float32
    wide = 2 * lanes
    length = reluctivity_table.shape[0]
    pieces = -(-length // 128)
    pad = (0, pieces * 128 - length)
    table = jnp.concatenate([jnp.pad(reluctivity_table, pad).reshape(pieces, 128),
                             jnp.pad(conductivity_table, pad).reshape(pieces, 128)])
    deep, tall = BA + 2 * HALO, rows + 8

    def landing(count, depth):
        return [
            pltpu.VMEM((2, count, depth, rows, wide), f32),
            pltpu.VMEM((2, count, BA // 2, 8, wide), f32),
            pltpu.VMEM((2, count, BA // 2, 8, wide), f32),
            pltpu.VMEM((4, count, HALO // 2, 8, wide), f32),
            pltpu.VMEM((4, count, HALO // 2, 8, wide), f32),
        ]

    vmem = pl.BlockSpec(memory_space=pltpu.VMEM)
    return pl.pallas_call(
        functools.partial(kernel, groups, radials),
        out_shape=(jax.ShapeDtypeStruct(source.shape, f32),) * 2,
        in_specs=[vmem] * 4,
        out_specs=(vmem, vmem),
        scratch_shapes=[
            pltpu.VMEM((6, layers, rows, lanes), f32),
            pltpu.VMEM((6, BA, rows, lanes), f32),
            pltpu.VMEM((6, deep, tall, wide), f32),
            pltpu.VMEM((3, deep, tall, wide), f32),
            pltpu.VMEM((deep, tall, wide), f32),
            pltpu.VMEM((deep, tall, wide), f32),
            pltpu.VMEM((deep, tall, wide), f32),
            pltpu.VMEM((1, deep, tall, wide), f32),
            pltpu.VMEM((3, BA, rows, wide), f32),
            pltpu.VMEM((2, 3, BA, rows, lanes), f32),
            pltpu.VMEM((2, 3, BA, rows, lanes), f32),
            pltpu.VMEM((1 + CYCLES, 16, 128), f32),
            pltpu.VMEM((1 + CYCLES, 3, groups, 16, 128), f32),
            pltpu.VMEM((groups + 2, 8, 128), f32),
            pltpu.VMEM((3, groups, 8, 128), f32),
            pltpu.VMEM((8, 128), f32),
            *landing(6, 3), *landing(3, 3), *landing(1, 4), *landing(1, 4),
            pltpu.SemaphoreType.DMA((4,)),
            pltpu.SemaphoreType.DMA((32,)),
            pltpu.SemaphoreType.DMA((32,)),
            pltpu.SemaphoreType.DMA((1 + CYCLES, 3, groups)),
            pltpu.SemaphoreType.DMA((1 + CYCLES, 3, groups)),
        ],
        compiler_params=pltpu.CompilerParams(
            collective_id=0, has_side_effects=True, vmem_limit_bytes=48 * 1024 * 1024),
    )(source, region, flags, table)


def solution(mesh):
    placed = (
        P(None, "axial", "radial", "azim"),
        P("axial", "radial", "azim"),
        P("axial", "radial", "azim"),
        P(),
        P(),
    )
    out = P(None, "axial", "radial", "azim")
    return jax.shard_map(
        functools.partial(on_device, 2 * mesh.shape["axial"], mesh.shape["radial"]),
        mesh=mesh,
        in_specs=placed,
        out_specs=(out, out),
        check_vma=False,
    )
```

time: 472 us -> 82 us (0.17)
  the two profiles are of different devices: /device:TPU:0 before, /device:TPU:5 now
where the time goes in v1:
time: 82 us; the launch traced here: 81.8 us
  Pallas kernels  76.1 us (93%)
  local copies, waits for them, and re-layouts  4.99 us (6%)
    pallas_call x1, Pallas kernels, on_device(): pl.pallas_call(functools.partial(kernel, groups, radials), out_shape=(jax...  76.1 us
    unnamed x8, local copies, waits for them, and re-layouts  4.29 us

profile of v1, /device:TPU:5, one launch (start us, length us, event | category | flops | bytes accessed | tf_op | source)
XLA Modules:
  0.0 81.8 jit_solution(2856618621348537976)
XLA Ops:
  0.6 0.7 pad_bitcast_fusion
  1.3 0.0 copy-start
  1.4 1.0 %copy-done = f32[3,16,16,128]{3,2,1,0:T(8,128)S(1)} copy-done((f32[3,16,16,128]{3,2,1,0:T(8,128)S(1)}, f32[3,16,16,128]{3,2,1,0:T(8,128)}, u32[]{:S(2)}) %copy-start) | copy-done | bytes 393240
  2.3 0.0 copy-start.1
  2.3 0.9 %copy-done.1 = s32[16,16,128]{2,1,0:T(8,128)S(1)} copy-done((s32[16,16,128]{2,1,0:T(8,128)S(1)}, s32[16,16,128]{2,1,0:T(8,128)}, u32[]{:S(2)}) %copy-start.1) | copy-done | bytes 131096
  3.2 0.0 copy-start.2
  3.2 0.9 %copy-done.2 = s32[16,16,128]{2,1,0:T(8,128)S(1)} copy-done((s32[16,16,128]{2,1,0:T(8,128)S(1)}, s32[16,16,128]{2,1,0:T(8,128)}, u32[]{:S(2)}) %copy-start.2) | copy-done | bytes 131096
  4.2 76.1 %shard_map.68 = (f32[3,16,16,128]{3,2,1,0:T(8,128)S(1)}, f32[3,16,16,128]{3,2,1,0:T(8,128)S(1)}) custom-call(f32[3,16,16,128]{3,2,1,0:T(8,128)S(1)} %copy-done, s32[16,16,128]{2,1,0:T(8,128)S(1)} %copy-done.1, s32[16,16,128]{2,1,0:T(8,128)S(1)} %copy-done.2, f32[8,128]{1,0:T(8,128)S(1)} %pad_maximum_fusion.table), custom_call_target="tpu_custom_call" | custom-call | tf_op jit(solution)/shard_map/pallas_call | solution.py:474
  80.3 0.7 copy.9
  81.1 0.7 copy.10
  (1 shorter events, 0.0 us)
Async XLA Ops:
  1.3 1.0 %copy-start = (f32[3,16,16,128]{3,2,1,0:T(8,128)S(1)}, f32[3,16,16,128]{3,2,1,0:T(8,128)}, u32[]{:S(2)}) copy-start(f32[3,16,16,128]{3,2,1,0:T(8,128)} %source.1) | copy-start | bytes 1179652
  2.3 0.9 %copy-start.1 = (s32[16,16,128]{2,1,0:T(8,128)S(1)}, s32[16,16,128]{2,1,0:T(8,128)}, u32[]{:S(2)}) copy-start(s32[16,16,128]{2,1,0:T(8,128)} %region.1) | copy-start | bytes 393220
  3.2 0.9 %copy-start.2 = (s32[16,16,128]{2,1,0:T(8,128)S(1)}, s32[16,16,128]{2,1,0:T(8,128)}, u32[]{:S(2)}) copy-start(s32[16,16,128]{2,1,0:T(8,128)} %flags.1) | copy-start | bytes 393220

commit v2 on v1

--- a/solution.py
+++ b/solution.py
@@ -24,8 +24,8 @@
 def kernel(groups, radials, source, region, flags, table, out_sol, out_res,
            pack, swap_in, main, inv, ninv, nres, chg, pot, sol, stage, fin,
            tot_out, tot_in, ysolve, pivs, ends,
-           ax0, rs0, rr0, cs0, cr0, ax1, rs1, rr1, cs1, cr1,
-           pa0, ps0, pr0, pcs0, pcr0, pa1, ps1, pr1, pcs1, pcr1,
+           ax0, rs0, rr0, co0, ax1, rs1, rr1, co1,
+           pa0, ps0, pr0, pc0, pa1, ps1, pr1, pc1,
            swap_sems, ex_send, ex_recv, tot_send, tot_recv):
     ax = lax.axis_index("axial")
     rd = lax.axis_index("radial")
@@ -122,9 +122,12 @@
     def turn(value):
         return pltpu.roll(value, 4, axis=0)
 
-    def swap_rows(fields, buf, count, depth, base):
-        axial, rsend, rrecv, csend, crecv = buf
-        copies = []
+    pair_of = lax.shift_right_logical(sub, 1)
+
+    def swap_rows(fields, buf, narrow, count, depth, base):
+        axial, rsend, rrecv, corner = buf
+        tiles = 2 * narrow + (BA // 2) * (count - narrow)
+        begun = []
 
         def send(index, da, dr, src, dst):
             copy = pltpu.make_async_remote_copy(
@@ -132,69 +135,92 @@
                 send_sem=ex_send.at[base + index], recv_sem=ex_recv.at[base + index],
                 device_id=device(mine + da, rd + dr), device_id_type=MESH)
             ok = exists(da, dr)
-            back = exists(-da, -dr)
             pl.when(ok)(lambda: copy.start())
-            copies.append((ok, back, copy))
-
-        send(0, 1, 0, fields.at[0:count, last - depth:last, 0:rows, :], axial.at[0])
-        send(1, -1, 0, fields.at[0:count, first:first + depth, 0:rows, :], axial.at[1])
-
-        def pack_rows(dst, layer_lo, half, dr):
+            return (ok, exists(-da, -dr), copy)
+
+        def wait_in(item):
+            pl.when(item[1])(lambda: item[2].wait_recv())
+
+        def wait_out(item):
+            pl.when(item[0])(lambda: item[2].wait_send())
+
+        for index, dr in ((0, 1), (1, -1)):
+            dst = rsend.at[index]
             top = rows - 8 if dr > 0 else 0
-
-            def body(pair, carry):
-                for field in range(count):
-                    a = fields[field, layer_lo + pair, top:top + 8, :]
-                    b = fields[field, layer_lo + half + pair, top:top + 8, :]
-                    if dr > 0:
-                        dst[field, pair] = jnp.where(low_half, turn(b), a)
-                    else:
-                        dst[field, pair] = jnp.where(low_half, a, turn(b))
-                return carry
-
-            lax.fori_loop(0, half, body, 0)
-
-        for index, dr in ((0, 1), (1, -1)):
-            pack_rows(rsend.at[index], first, BA // 2, dr)
-            send(2 + index, 0, dr, rsend.at[index], rrecv.at[index])
-        slot = 0
-        for da in (1, -1):
-            for dr in (1, -1):
-                lo = last - HALO if da > 0 else first
-                pack_rows(csend.at[slot], lo, HALO // 2, dr)
-                send(4 + slot, da, dr, csend.at[slot], crecv.at[slot])
-                slot += 1
+            for field in range(narrow):
+                for tile in range(2):
+                    value = fields[field, first + tile, top:top + 8, :]
+                    for step in range(1, 4):
+                        more = fields[field, first + tile + 2 * step, top:top + 8, :]
+                        spot = 3 - step if dr > 0 else step
+                        more = pltpu.roll(more, 8 - 2 * step if dr > 0 else 2 * step, axis=0)
+                        value = jnp.where(pair_of == spot, more, value)
+                    dst[2 * field + tile] = value
+            if narrow and dr > 0:
+                value = fields[1, first + 5, top:top + 8, :]
+                for layer in range(BA):
+                    if layer != 5:
+                        more = pltpu.roll(fields[1, first + layer, top:top + 8, :], (layer + 3) % 8, axis=0)
+                        value = jnp.where(sub == layer, more, value)
+                dst[tiles] = value
+            for field in range(narrow, count):
+                for pair in range(BA // 2):
+                    a = fields[field, first + pair, top:top + 8, :]
+                    b = turn(fields[field, first + BA // 2 + pair, top:top + 8, :])
+                    at = 2 * narrow + (BA // 2) * (field - narrow) + pair
+                    dst[at] = jnp.where(low_half, b, a) if dr > 0 else jnp.where(low_half, a, b)
+            size = tiles + 1 if narrow and dr > 0 else tiles
+            begun.append(send(2 + index, 0, dr, rsend.at[index, 0:size], rrecv.at[index, 0:size]))
+
+        begun.append(send(0, 1, 0, fields.at[0:count, last - depth:last, 0:rows, :], axial.at[0]))
+        begun.append(send(1, -1, 0, fields.at[0:count, first:first + depth, 0:rows, :], axial.at[1]))
 
         def finish():
-            for ok, back, copy in copies:
-                pl.when(ok)(lambda copy=copy: copy.wait_send())
-                pl.when(back)(lambda copy=copy: copy.wait_recv())
-            for index, da in ((0, -1), (1, 1)):
-                ok = exists(da, 0)
-
-                def body(layer, carry, index=index, da=da, ok=ok):
-                    to = layer + (first - depth if da < 0 else last)
-                    for field in range(count):
-                        fields[field, to, 0:rows, :] = jnp.where(ok, axial[index, field, layer], 0.0)
-                    return carry
-
-                lax.fori_loop(0, depth, body, 0)
-
-            def unpack(from_low, from_up, low_ok, up_ok, layer_lo, half):
-                def body(pair, carry):
-                    for field in range(count):
-                        down = jnp.where(low_ok, from_low[field, pair], 0.0)
-                        up = jnp.where(up_ok, from_up[field, pair], 0.0)
-                        fields[field, layer_lo + pair, rows:frame_rows, :] = jnp.where(low_half, up, down)
-                        fields[field, layer_lo + half + pair, rows:frame_rows, :] = turn(
-                            jnp.where(low_half, down, up))
-                    return carry
-
-                lax.fori_loop(0, half, body, 0)
-
-            unpack(rrecv.at[0], rrecv.at[1], exists(0, -1), exists(0, 1), first, BA // 2)
-            unpack(crecv.at[0], crecv.at[1], exists(-1, -1), exists(-1, 1), first - HALO, HALO // 2)
-            unpack(crecv.at[2], crecv.at[3], exists(1, -1), exists(1, 1), last, HALO // 2)
+            wait_in(begun[0])
+            wait_in(begun[1])
+            low_ok, up_ok = exists(0, -1), exists(0, 1)
+            low, up = rrecv.at[0], rrecv.at[1]
+            for field in range(narrow):
+                for tile in range(2):
+                    down = jnp.where(low_ok, low[2 * field + tile], 0.0)
+                    above = jnp.where(up_ok, up[2 * field + tile], 0.0)
+                    for step in range(4):
+                        layer = tile + 2 * step
+                        d = pltpu.roll(down, 2 * step, axis=0) if step else down
+                        u = pltpu.roll(above, 8 - 2 * step, axis=0) if step else above
+                        value = jnp.where(sub < 2, u, d)
+                        if field == 1:
+                            extra = jnp.where(low_ok, low[tiles], 0.0)
+                            if layer != 5:
+                                extra = pltpu.roll(extra, (5 - layer) % 8, axis=0)
+                            value = jnp.where(sub == 5, extra, value)
+                        fields[field, first + layer, rows:frame_rows, :] = value
+            for field in range(narrow, count):
+                for pair in range(BA // 2):
+                    at = 2 * narrow + (BA // 2) * (field - narrow) + pair
+                    down = jnp.where(low_ok, low[at], 0.0)
+                    above = jnp.where(up_ok, up[at], 0.0)
+                    fields[field, first + pair, rows:frame_rows, :] = jnp.where(low_half, above, down)
+                    fields[field, first + BA // 2 + pair, rows:frame_rows, :] = turn(
+                        jnp.where(low_half, down, above))
+            begun.append(send(4, 1, 0, fields.at[0:count, last - depth:last, rows:frame_rows, :], corner.at[0]))
+            begun.append(send(5, -1, 0, fields.at[0:count, first:first + depth, rows:frame_rows, :], corner.at[1]))
+            for part, at in ((2, 0), (4, rows)):
+                for index, da in ((0, -1), (1, 1)):
+                    wait_in(begun[part + index])
+                    ok = exists(da, 0)
+                    buffer = axial if part == 2 else corner
+                    to = first - depth if da < 0 else last
+
+                    def body(layer, carry, index=index, ok=ok, buffer=buffer, to=to, at=at):
+                        for field in range(count):
+                            fields[field, to + layer, at:(rows if at == 0 else frame_rows), :] = jnp.where(
+                                ok, buffer[index, field, layer], 0.0)
+                        return carry
+
+                    lax.fori_loop(0, depth, body, 0)
+            for item in begun:
+                wait_out(item)
 
         return finish
 
@@ -241,8 +267,8 @@
         right = jnp.sum(value[:, lanes:wide], keepdims=True)
         return jnp.where(odd, jnp.broadcast_to(right, (8, 128)), jnp.broadcast_to(left, (8, 128)))
 
-    bufs_main = (ax0, rs0, rr0, cs0, cr0)
-    finish_main = swap_rows(main, bufs_main, 6, 3, 0)
+    bufs_main = (ax0, rs0, rr0, co0)
+    finish_main = swap_rows(main, bufs_main, 3, 6, 3, 0)
     tot_out[0, 0:8] = halves(main[4, last - 1, 0:rows, :])
     tot_out[0, 8:16] = ground_share * halves(main[4, first, 0:rows, :])
     finish_coef = share(0)
@@ -351,7 +377,7 @@
 
     for cycle in range(CYCLES):
         if cycle:
-            swap_rows(main, (ax1, rs1, rr1, cs1, cr1), 3, 3, 8)()
+            swap_rows(main, (ax1, rs1, rr1, co1), 3, 3, 3, 8)()
 
         def node(layer, carry):
             r0, r1, r2 = main[0, layer], main[1, layer], main[2, layer]
@@ -379,8 +405,8 @@
 
         lax.fori_loop(first - 1, last + 1, advance, 0)
 
-        bufs_pot = (pa0, ps0, pr0, pcs0, pcr0) if cycle == 0 else (pa1, ps1, pr1, pcs1, pcr1)
-        finish_pot = swap_rows(pot, bufs_pot, 1, 4, 16 + 8 * cycle)
+        bufs_pot = (pa0, ps0, pr0, pc0) if cycle == 0 else (pa1, ps1, pr1, pc1)
+        finish_pot = swap_rows(pot, bufs_pot, 0, 1, 4, 16 + 8 * cycle)
 
         def total(layer, carry):
             flux, acc = carry
@@ -461,13 +487,13 @@
                              jnp.pad(conductivity_table, pad).reshape(pieces, 128)])
     deep, tall = BA + 2 * HALO, rows + 8
 
-    def landing(count, depth):
+    def landing(narrow, count, depth):
+        tiles = 2 * narrow + (BA // 2) * (count - narrow) + (1 if narrow else 0)
         return [
             pltpu.VMEM((2, count, depth, rows, wide), f32),
-            pltpu.VMEM((2, count, BA // 2, 8, wide), f32),
-            pltpu.VMEM((2, count, BA // 2, 8, wide), f32),
-            pltpu.VMEM((4, count, HALO // 2, 8, wide), f32),
-            pltpu.VMEM((4, count, HALO // 2, 8, wide), f32),
+            pltpu.VMEM((2, tiles, 8, wide), f32),
+            pltpu.VMEM((2, tiles, 8, wide), f32),
+            pltpu.VMEM((2, count, depth, 8, wide), f32),
         ]
 
     vmem = pl.BlockSpec(memory_space=pltpu.VMEM)
@@ -493,7 +519,7 @@
             pltpu.VMEM((groups + 2, 8, 128), f32),
             pltpu.VMEM((3, groups, 8, 128), f32),
             pltpu.VMEM((8, 128), f32),
-            *landing(6, 3), *landing(3, 3), *landing(1, 4), *landing(1, 4),
+            *landing(3, 6, 3), *landing(3, 3, 3), *landing(0, 1, 4), *landing(0, 1, 4),
             pltpu.SemaphoreType.DMA((4,)),
             pltpu.SemaphoreType.DMA((32,)),
             pltpu.SemaphoreType.DMA((32,)),

time: 82 us -> 72 us (0.88)
  Pallas kernels: 76.1 us -> 66.1 us
    pallas_call x1, Pallas kernels: 76.1 us -> 66.1 us  [on_device(): pl.pallas_call(functools.partial(kernel, groups, radials), out_shape=(jax...]
where the time goes in v2:
time: 72 us; the launch traced here: 71.8 us
  Pallas kernels  66.1 us (92%)
  local copies, waits for them, and re-layouts  4.99 us (7%)
    pallas_call x1, Pallas kernels, on_device(): pl.pallas_call(functools.partial(kernel, groups, radials), out_shape=(jax...  66.1 us
    unnamed x8, local copies, waits for them, and re-layouts  4.29 us

profile of v2, /device:TPU:5, one launch (start us, length us, event | category | flops | bytes accessed | tf_op | source)
XLA Modules:
  0.0 71.8 jit_solution(12337087199872927373)
XLA Ops:
  0.6 0.7 pad_bitcast_fusion
  1.3 0.0 copy-start
  1.4 1.0 %copy-done = f32[3,16,16,128]{3,2,1,0:T(8,128)S(1)} copy-done((f32[3,16,16,128]{3,2,1,0:T(8,128)S(1)}, f32[3,16,16,128]{3,2,1,0:T(8,128)}, u32[]{:S(2)}) %copy-start) | copy-done | bytes 393240
  2.3 0.0 copy-start.1
  2.3 0.9 %copy-done.1 = s32[16,16,128]{2,1,0:T(8,128)S(1)} copy-done((s32[16,16,128]{2,1,0:T(8,128)S(1)}, s32[16,16,128]{2,1,0:T(8,128)}, u32[]{:S(2)}) %copy-start.1) | copy-done | bytes 131096
  3.2 0.0 copy-start.2
  3.2 0.9 %copy-done.2 = s32[16,16,128]{2,1,0:T(8,128)S(1)} copy-done((s32[16,16,128]{2,1,0:T(8,128)S(1)}, s32[16,16,128]{2,1,0:T(8,128)}, u32[]{:S(2)}) %copy-start.2) | copy-done | bytes 131096
  4.2 66.1 %shard_map.68 = (f32[3,16,16,128]{3,2,1,0:T(8,128)S(1)}, f32[3,16,16,128]{3,2,1,0:T(8,128)S(1)}) custom-call(f32[3,16,16,128]{3,2,1,0:T(8,128)S(1)} %copy-done, s32[16,16,128]{2,1,0:T(8,128)S(1)} %copy-done.1, s32[16,16,128]{2,1,0:T(8,128)S(1)} %copy-done.2, f32[8,128]{1,0:T(8,128)S(1)} %pad_maximum_fusion.table), custom_call_target="tpu_custom_call" | custom-call | tf_op jit(solution)/shard_map/pallas_call | solution.py:500
  70.3 0.7 %copy.9 = f32[3,16,16,128]{3,2,1,0:T(8,128)} copy(f32[3,16,16,128]{3,2,1,0:T(8,128)S(1)} %get-tuple-element.6) | data formatting | bytes 786432
  71.0 0.7 %copy.10 = f32[3,16,16,128]{3,2,1,0:T(8,128)} copy(f32[3,16,16,128]{3,2,1,0:T(8,128)S(1)} %get-tuple-element.7) | data formatting | bytes 786432
  (1 shorter events, 0.0 us)
Async XLA Ops:
  1.3 1.0 %copy-start = (f32[3,16,16,128]{3,2,1,0:T(8,128)S(1)}, f32[3,16,16,128]{3,2,1,0:T(8,128)}, u32[]{:S(2)}) copy-start(f32[3,16,16,128]{3,2,1,0:T(8,128)} %source.1) | copy-start | bytes 1179652
  2.3 0.9 %copy-start.1 = (s32[16,16,128]{2,1,0:T(8,128)S(1)}, s32[16,16,128]{2,1,0:T(8,128)}, u32[]{:S(2)}) copy-start(s32[16,16,128]{2,1,0:T(8,128)} %region.1) | copy-start | bytes 393220
  3.2 0.9 %copy-start.2 = (s32[16,16,128]{2,1,0:T(8,128)S(1)}, s32[16,16,128]{2,1,0:T(8,128)}, u32[]{:S(2)}) copy-start(s32[16,16,128]{2,1,0:T(8,128)} %flags.1) | copy-start | bytes 393220

commit v3 on v2

--- a/solution.py
+++ b/solution.py
@@ -12,6 +12,7 @@
 NS = 2
 ES = 2
 HALO = 4
+UNROLL = True
 MESH = pl.DeviceIdType.MESH
 
 relax_edge = 0.4
@@ -19,6 +20,10 @@
 ground_share = 0.01
 
 NEIGHBOURS = [(0, -1), (0, 1), (-1, 0), (1, 0), (-1, -1), (-1, 1), (1, -1), (1, 1)]
+
+
+def steps(low, high, body, carry):
+    return lax.fori_loop(low, high, body, carry, unroll=UNROLL)
 
 
 def kernel(groups, radials, source, region, flags, table, out_sol, out_res,
@@ -92,7 +97,7 @@
         pack[5, layer] = free
         return carry
 
-    lax.fori_loop(0, own_layers, look, 0)
+    steps(0, own_layers, look, 0)
 
     columns = 1 + (rd > 0).astype(jnp.int32) + (rd < radials - 1).astype(jnp.int32)
     pl.semaphore_wait(barrier, columns * groups - 1)
@@ -114,7 +119,7 @@
             main[field, first + layer, 0:rows, lanes:wide] = jnp.where(is_low, there, here)
         return carry
 
-    lax.fori_loop(0, BA, place, 0)
+    steps(0, BA, place, 0)
 
     sub = lax.broadcasted_iota(jnp.int32, (8, wide), 0)
     low_half = sub < 4
@@ -218,7 +223,7 @@
                                 ok, buffer[index, field, layer], 0.0)
                         return carry
 
-                    lax.fori_loop(0, depth, body, 0)
+                    steps(0, depth, body, 0)
             for item in begun:
                 wait_out(item)
 
@@ -299,7 +304,7 @@
         ninv[layer] = jnp.where(inside, relax_node / jnp.where(inside, nodes, 1.0), 0.0)
         return carry
 
-    lax.fori_loop(first - 2, last + 2, setup, 0)
+    steps(first - 2, last + 2, setup, 0)
 
     finish_coef()
     previous = None
@@ -353,7 +358,7 @@
         b0, b1, b2 = edges(lo - 1)
         c0, c1, c2 = edges(lo)
         _, h1, h2 = fields_of(lo - 1, b0, b1, b2, c1, c2)
-        lax.fori_loop(lo, hi, body, (c0, c1, c2, h1, h2))
+        steps(lo, hi, body, (c0, c1, c2, h1, h2))
 
     def corrections(layer):
         p = pot[0, layer]
@@ -386,7 +391,7 @@
             chg[layer] = ninv[layer] * value
             return carry
 
-        lax.fori_loop(first - 2, last + 2, node, 0)
+        steps(first - 2, last + 2, node, 0)
 
         def second(layer, flux):
             value, flux = laplace(layer, flux)
@@ -395,7 +400,7 @@
             pot[0, layer] = chg[layer]
             return flux
 
-        lax.fori_loop(first - 1, last + 1, second, low_flux_of(first - 2))
+        steps(first - 1, last + 1, second, low_flux_of(first - 2))
 
         def advance(layer, carry):
             change = ninv[layer] * nres[layer]
@@ -403,7 +408,7 @@
             pot[0, layer] = pot[0, layer] + change
             return carry
 
-        lax.fori_loop(first - 1, last + 1, advance, 0)
+        steps(first - 1, last + 1, advance, 0)
 
         bufs_pot = (pa0, ps0, pr0, pc0) if cycle == 0 else (pa1, ps1, pr1, pc1)
         finish_pot = swap_rows(pot, bufs_pot, 0, 1, 4, 16 + 8 * cycle)
@@ -413,7 +418,7 @@
             value, flux = laplace(layer, flux)
             return flux, acc + (nres[layer] - value)[0:rows]
 
-        _, acc = lax.fori_loop(first, last, total,
+        _, acc = steps(first, last, total,
                                (low_flux_of(first - 1), jnp.zeros((rows, wide), jnp.float32)))
         tot_out[1 + cycle, 0:8] = halves(acc)
         tot_out[1 + cycle, 8:16] = jnp.zeros((8, 128), jnp.float32)
@@ -444,7 +449,7 @@
                 pot[0, layer] = pot[0, layer] + spread
                 return carry
 
-            lax.fori_loop(lo, hi, lift, 0)
+            steps(lo, hi, lift, 0)
 
         sweep(first - 2, last + 2, corrections, cycle == 0)
         sweep(first - 1, last + 1, relaxed, False)
@@ -460,7 +465,7 @@
                 stage[which, comp, layer] = jnp.where(is_low, right, left)
         return carry
 
-    lax.fori_loop(0, BA, split, 0)
+    steps(0, BA, split, 0)
     final = pltpu.make_async_remote_copy(
         src_ref=stage, dst_ref=fin, send_sem=swap_sems.at[2], recv_sem=swap_sems.at[3],
         device_id={"axial": ax, "radial": rd, "azim": other}, device_id_type=MESH)
@@ -473,7 +478,7 @@
             out_res[comp, other * BA + layer] = fin[1, comp, layer]
         return carry
 
-    lax.fori_loop(0, BA, fetch, 0)
+    steps(0, BA, fetch, 0)
 
 
 def on_device(groups, radials, source, region, flags, reluctivity_table, conductivity_table):

time: 72 us -> 59.1 us (0.82)
  Pallas kernels: 66.1 us -> 53.2 us
    pallas_call x1, Pallas kernels: 66.1 us -> 53.2 us  [on_device(): pl.pallas_call(functools.partial(kernel, groups, radials), out_shape=(jax...]
where the time goes in v3:
time: 59.1 us; the launch traced here: 58.9 us
  Pallas kernels  53.2 us (90%)
  local copies, waits for them, and re-layouts  4.99 us (8%)
  between operations  0.65 us (1%)
    pallas_call x1, Pallas kernels, on_device(): pl.pallas_call(functools.partial(kernel, groups, radials), out_shape=(jax...  53.2 us
    unnamed x8, local copies, waits for them, and re-layouts  4.29 us

profile of v3, /device:TPU:5, one launch (start us, length us, event | category | flops | bytes accessed | tf_op | source)
XLA Modules:
  0.0 58.9 jit_solution(17529318012154013647)
XLA Ops:
  0.6 0.7 %pad_bitcast_fusion = (f32[4,128]{1,0:T(4,128)S(1)}, f32[4,128]{1,0:T(4,128)S(1)}) fusion(f32[402]{0:T(512)} %param.9, f32[402]{0:T(512)} %param.8), kind=kLoop, calls=%fused_computation.1 | loop fusion | bytes 7312 | tf_op jit(solution)/shard_map/reshape | solution.py:492
  1.3 0.0 copy-start
  1.4 1.0 %copy-done = f32[3,16,16,128]{3,2,1,0:T(8,128)S(1)} copy-done((f32[3,16,16,128]{3,2,1,0:T(8,128)S(1)}, f32[3,16,16,128]{3,2,1,0:T(8,128)}, u32[]{:S(2)}) %copy-start) | copy-done | bytes 393240
  2.3 0.0 copy-start.1
  2.3 0.9 %copy-done.1 = s32[16,16,128]{2,1,0:T(8,128)S(1)} copy-done((s32[16,16,128]{2,1,0:T(8,128)S(1)}, s32[16,16,128]{2,1,0:T(8,128)}, u32[]{:S(2)}) %copy-start.1) | copy-done | bytes 131096
  3.2 0.0 copy-start.2
  3.2 0.9 %copy-done.2 = s32[16,16,128]{2,1,0:T(8,128)S(1)} copy-done((s32[16,16,128]{2,1,0:T(8,128)S(1)}, s32[16,16,128]{2,1,0:T(8,128)}, u32[]{:S(2)}) %copy-start.2) | copy-done | bytes 131096
  4.2 53.2 %shard_map.68 = (f32[3,16,16,128]{3,2,1,0:T(8,128)S(1)}, f32[3,16,16,128]{3,2,1,0:T(8,128)S(1)}) custom-call(f32[3,16,16,128]{3,2,1,0:T(8,128)S(1)} %copy-done, s32[16,16,128]{2,1,0:T(8,128)S(1)} %copy-done.1, s32[16,16,128]{2,1,0:T(8,128)S(1)} %copy-done.2, f32[8,128]{1,0:T(8,128)S(1)} %pad_maximum_fusion.table), custom_call_target="tpu_custom_call" | custom-call | tf_op jit(solution)/shard_map/pallas_call | solution.py:505
  57.4 0.7 %copy.9 = f32[3,16,16,128]{3,2,1,0:T(8,128)} copy(f32[3,16,16,128]{3,2,1,0:T(8,128)S(1)} %get-tuple-element.6) | data formatting | bytes 786432
  58.1 0.7 %copy.10 = f32[3,16,16,128]{3,2,1,0:T(8,128)} copy(f32[3,16,16,128]{3,2,1,0:T(8,128)S(1)} %get-tuple-element.7) | data formatting | bytes 786432
  (1 shorter events, 0.0 us)
Async XLA Ops:
  1.3 1.0 %copy-start = (f32[3,16,16,128]{3,2,1,0:T(8,128)S(1)}, f32[3,16,16,128]{3,2,1,0:T(8,128)}, u32[]{:S(2)}) copy-start(f32[3,16,16,128]{3,2,1,0:T(8,128)} %source.1) | copy-start | bytes 1179652
  2.3 0.9 %copy-start.1 = (s32[16,16,128]{2,1,0:T(8,128)S(1)}, s32[16,16,128]{2,1,0:T(8,128)}, u32[]{:S(2)}) copy-start(s32[16,16,128]{2,1,0:T(8,128)} %region.1) | copy-start | bytes 393220
  3.2 0.9 %copy-start.2 = (s32[16,16,128]{2,1,0:T(8,128)S(1)}, s32[16,16,128]{2,1,0:T(8,128)}, u32[]{:S(2)}) copy-start(s32[16,16,128]{2,1,0:T(8,128)} %flags.1) | copy-start | bytes 393220
